TPU v7x, 128 devices: a whole 4x4x4 slice. The times are simulated.
128 devices in a mesh: rep: 4 (over y_lo, core), fsdp: 32 (over z, x, y_hi).
Axes of the slice: x: 4, y: 4 (y_hi: 2, y_lo: 2; y = y_hi * 2 + y_lo), z: 4, core: 2. Of those that a mesh axis runs over, the one named last changes fastest.
Arguments:
- inputs: bfloat16 [4, 12288, 2304], P('rep', 'fsdp'), may hold values from -6 to 6
- cotangent: bfloat16 [4, 12288, 4608], P('rep', 'fsdp'), may hold values from -6 to 6
- params: float32 [4, 2304, 4608], P('rep', 'fsdp'), may hold values from -5 to 5
- first_moment: float32 [4, 2304, 4608], P('rep', 'fsdp'), may hold values from -5 to 5
- second_moment: float32 [4, 2304, 4608], P('rep', 'fsdp'), may hold values from 0.3 to 3
- snapshot: float32 [2304, 1152], P('fsdp'), may hold values from -5 to 5
- momentum: float32 [2304, 1152], P('fsdp'), may hold values from -4 to 4
- fragment: int32 [4], replicated, may hold values from 0 to 3, each once
Outputs:
- new_params: float32 [4, 2304, 4608], P('rep', 'fsdp')
- new_first: float32 [4, 2304, 4608], P('rep', 'fsdp')
- new_second: float32 [4, 2304, 4608], P('rep', 'fsdp')
- input_grad: bfloat16 [4, 12288, 2304], P('rep', 'fsdp')
- new_momentum: float32 [2304, 1152], P('fsdp')
- new_snapshot: float32 [2304, 1152], P('fsdp')
Inputs may be any that keep to these rules, and one draw needn't show every extreme that they name: Each fragment appears once; fragment[0] is the fragment whose outer step this window takes.
All inputs are finite; a program needn't handle non-finite values.
Results may differ from a plain program's by a relative error of at most 0.023.
Values may be sent and summed in bfloat16 or wider, within the bound.
A program may use at most 192 MiB of HBM per device.

v0:
```python
import jax
import jax.numpy as jnp
from jax import lax
from jax.sharding import PartitionSpec as P

beta_one = 0.9
beta_two = 0.95
inner_rate = 0.01
adam_eps = 1e-08
decay_rate = 0.1
outer_rate = 0.7
outer_mu = 0.9
mix_rate = 0.5


def gelu_cot(pre, cot):
    return jax.vjp(lambda t: jax.nn.gelu(t, approximate=True), pre)[1](cot)[0]


def outer_update(weights, snapshot, momentum, start_col):
    local = lax.dynamic_slice_in_dim(weights, start_col, snapshot.shape[1], 1)
    total = lax.psum((snapshot - local).astype(jnp.bfloat16), "rep").astype(jnp.float32)
    outer_grad = total / lax.axis_size("rep")
    new_momentum = outer_mu * momentum + outer_grad
    new_snapshot = snapshot - outer_rate * (outer_grad + outer_mu * new_momentum)
    return (new_momentum, new_snapshot)


def body(inputs, cotangent, params, first_moment, second_moment, snapshot, momentum, fragment):
    acts = inputs[0]
    weights = params[0]
    scale = acts.shape[1] ** (-0.5)
    start_col = fragment[0] * snapshot.shape[1]
    shard_low = weights.astype(jnp.bfloat16)
    whole = lax.all_gather(shard_low, "fsdp", axis=0, tiled=True)
    pre = jnp.dot(acts, whole, preferred_element_type=jnp.float32) * scale
    hidden_cot = (gelu_cot(pre, cotangent[0].astype(jnp.float32)) * scale).astype(jnp.bfloat16)
    back = lax.dot_general(
        hidden_cot, whole, (((1,), (1,)), ((), ())), preferred_element_type=jnp.float32
    )
    grad = lax.psum_scatter(
        lax.dot_general(
            acts, hidden_cot, (((0,), (0,)), ((), ())), preferred_element_type=jnp.float32
        ).astype(jnp.bfloat16),
        "fsdp",
        scatter_dimension=0,
        tiled=True,
    ).astype(jnp.float32)
    input_grad = back.astype(jnp.bfloat16)[None]
    first = beta_one * first_moment[0] + (1.0 - beta_one) * grad
    second = beta_two * second_moment[0] + (1.0 - beta_two) * grad * grad
    stepped = weights - inner_rate * (first / (jnp.sqrt(second) + adam_eps) + decay_rate * weights)
    new_momentum, new_snapshot = outer_update(weights, snapshot, momentum, start_col)
    frag_part = lax.dynamic_slice_in_dim(stepped, start_col, snapshot.shape[1], 1)
    merged = mix_rate * new_snapshot + (1.0 - mix_rate) * frag_part
    stepped = lax.dynamic_update_slice_in_dim(stepped, merged, start_col, 1)
    return (stepped[None], first[None], second[None], input_grad, new_momentum, new_snapshot)


def solution(mesh):
    return jax.shard_map(
        body,
        mesh=mesh,
        in_specs=(
            P("rep", "fsdp", None),
            P("rep", "fsdp", None),
            P("rep", "fsdp", None),
            P("rep", "fsdp", None),
            P("rep", "fsdp", None),
            P("fsdp", None),
            P("fsdp", None),
            P(),
        ),
        out_specs=(
            P("rep", "fsdp", None),
            P("rep", "fsdp", None),
            P("rep", "fsdp", None),
            P("rep", "fsdp", None),
            P("fsdp", None),
            P("fsdp", None),
        ),
        check_vma=False,
    )
```

profile of v0, /device:TPU:0, one launch (start us, length us, event | category | flops | bytes accessed | tf_op | source)
XLA Modules:
  0.0 562.2 jit_solution(5974342191672632006)
XLA Ops:
  8.0 0.0 copy-start
  8.0 0.0 all-gather.2.cloned.1.call-start
  8.1 2.3 bitcast_convert_fusion
  10.4 0.0 all-gather.2.cloned.1.call-update
  10.4 0.0 reduce-scatter.4.cloned.1.call-start
  10.5 187.3 %all-gather.2.cloned.1.call-done = bf16[2304,4608]{1,0:T(8,128)(2,1)} async-done(((bf16[72,4608]{1,0:T(8,128)(2,1)}), bf16[2304,4608]{1,0:T(8,128)(2,1)}) %all-gather.2.cloned.1.call-update) | async-done | bytes 21233680 | tf_op jit(solution)/shard_map/all_gather | solution.py:35
  197.8 0.0 copy-done
  197.8 17.2 %fusion.4 = bf16[384,4608]{1,0:T(8,128)(2,1)S(1)} fusion(bf16[2304,4608]{1,0:T(8,128)(2,1)} %all-gather.2.cloned.1.call-done, bf16[1,384,4608]{2,1,0:T(8,128)(2,1)} %param.9, bf16[1,384,2304]{2,1,0:T(8,128)(2,1)S(1)} %copy-done), kind=kOutput, calls=%fused_computation.10 | convolution fusion | flops 8194424832 | bytes 30081024 | tf_op jit(solution)/shard_map/dot_general | solution.py:36
  215.0 0.0 copy-start.7
  215.0 1.8 copy-done.7
  216.8 14.6 %fusion = bf16[2304,4608]{0,1:T(8,128)(2,1)} fusion(bf16[384,4608]{1,0:T(8,128)(2,1)S(1)} %fusion.4, bf16[1,384,2304]{2,1,0:T(8,128)(2,1)S(1)} %copy-done), kind=kOutput, calls=%fused_computation.1 | convolution fusion | flops 8164343808 | bytes 26542080 | tf_op jit(solution)/shard_map/dot_general | solution.py:42
  231.3 28.4 %copy.27 = bf16[2304,4608]{1,0:T(8,128)(2,1)} copy(bf16[2304,4608]{0,1:T(8,128)(2,1)} %fusion) | data formatting | bytes 42467328
  259.7 0.0 copy-start.6
  259.7 0.0 copy-start.2
  259.7 0.0 copy-start.5
  259.7 0.0 reduce-scatter.4.cloned.1.call-update
  259.8 0.2 all-reduce.2.cloned.1.call-start
  260.0 0.4 copy-done.6
  260.4 0.6 copy-done.2
  261.1 0.1 copy-done.5
  261.1 0.7 fusion.21
  261.8 0.0 all-reduce.2.cloned.1.call-update
  261.9 15.5 %fusion.12 = bf16[1,384,2304]{2,1,0:T(8,128)(2,1)} fusion(bf16[384,4608]{1,0:T(8,128)(2,1)} %copy-done.7, bf16[2304,4608]{1,0:T(8,128)(2,1)} %all-gather.2.cloned.1.call-done), kind=kOutput, calls=%fused_computation.19 | convolution fusion | flops 8154611712 | bytes 26542080 | tf_op jit(solution)/shard_map/dot_general | solution.py:38
  277.3 268.6 %reduce-scatter.4.cloned.1.call-done = bf16[72,4608]{1,0:T(8,128)(2,1)} async-done(((bf16[2304,4608]{1,0:T(8,128)(2,1)}), bf16[72,4608]{1,0:T(8,128)(2,1)}) %reduce-scatter.4.cloned.1.call-update) | async-done | bytes 663568 | tf_op jit(solution)/shard_map/reduce_scatter | solution.py:41
  545.9 0.0 copy-start.1
  545.9 4.5 fusion.20
  550.4 0.0 copy-start.3
  550.4 1.1 copy-done.3
  551.5 0.1 copy.30
  551.6 0.0 all-reduce.2.cloned.1.call-done
  551.6 2.1 bitcast_dynamic-update-slice_fusion
  553.7 0.0 copy-start.4
  553.7 1.1 copy-done.4
  554.8 0.0 copy-done.1
Async XLA Ops:
  8.0 189.8 %copy-start = (bf16[1,384,2304]{2,1,0:T(8,128)(2,1)S(1)}, bf16[1,384,2304]{2,1,0:T(8,128)(2,1)}, u32[]{:S(2)}) copy-start(bf16[1,384,2304]{2,1,0:T(8,128)(2,1)} %param.8) | copy-start | bytes 5308420
  8.0 189.8 %all-gather.2.cloned.1.call-start = ((), (), s32[]{:S(2)}) async-start(), calls=%async_computation.1 | async-start | bytes 21897216 | tf_op jit(solution)/shard_map/all_gather | solution.py:35
  10.4 535.5 %reduce-scatter.4.cloned.1.call-start = ((), (), s32[]{:S(2)}) async-start(), calls=%async_computation.3 | async-start | bytes 21897216 | tf_op jit(solution)/shard_map/reduce_scatter | solution.py:41
  215.0 1.8 copy-start.7
  259.7 0.7 copy-start.6
  259.7 1.3 copy-start.2
  259.7 1.4 copy-start.5
  259.8 291.9 %all-reduce.2.cloned.1.call-start = ((), (), s32[]{:S(2)}) async-start(), calls=%async_computation.2 | async-start | bytes 331776 | tf_op jit(solution)/shard_map/psum | solution.py:22
  545.9 8.9 %copy-start.1 = (bf16[1,384,2304]{2,1,0:T(8,128)(2,1)S(1)}, bf16[1,384,2304]{2,1,0:T(8,128)(2,1)}, u32[]{:S(2)}) copy-start(bf16[1,384,2304]{2,1,0:T(8,128)(2,1)} %param.8) | copy-start | bytes 5308420
  550.4 1.1 copy-start.3
  553.7 1.1 copy-start.4
Sparse Core Ops, SparseCore 0:
  12.4 185.3 all-gather.1
  259.9 286.0 reduce-scatter.3
Sparse Core Ops, SparseCore 1:
  263.3 35.7 all-reduce.1
where the time goes:
time: 563 us; the launch traced here: 562 us
  waiting for transfers between devices  456 us (81%)
  matrix products  47.2 us (8%)
  local copies, waits for them, and re-layouts  33.5 us (6%)
  between operations  15.6 us (3%)
  other arithmetic  9.66 us (2%)
    reduce_scatter x1, waiting for transfers between devices, body(): lax.psum_scatter(lax.dot_general(acts, hidden_cot, (((0,), (0,)), ((), ()...  269 us
    all_gather x1, waiting for transfers between devices, body(): whole = lax.all_gather(shard_low, 'fsdp', axis=0, tiled=True)  187 us
    unnamed x18, local copies, waits for them, and re-layouts  33.5 us
    dot_general x1, matrix products, body(): pre = jnp.dot(acts, whole, preferred_element_type=jnp.float32) * scale  17.2 us
    dot_general x1, matrix products, body(): lax.dot_general(hidden_cot, whole, (((1,), (1,)), ((), ())), preferred_el...  15.5 us
    dot_general x1, matrix products, body(): lax.dot_general(acts, hidden_cot, (((0,), (0,)), ((), ())), preferred_ele...  14.6 us
  transfers between devices with their start and end apart: 3, of which 2 were waited for; matrix products, arithmetic and copies ran while one was open for 4% of the time, Pallas kernels for 0%

commit v1 on v0

v1 whole, which is shorter than its diff:
```python
import functools

import jax
import jax.numpy as jnp
from jax import lax
from jax.experimental import pallas as pl
from jax.experimental.pallas import tpu as pltpu
from jax.sharding import PartitionSpec as P

beta_one = 0.9
beta_two = 0.95
inner_rate = 0.01
adam_eps = 1e-08
decay_rate = 0.1
outer_rate = 0.7
outer_mu = 0.9
mix_rate = 0.5

LANES = 128
CHUNK = 256
MESH = pl.DeviceIdType.MESH
f32 = jnp.float32
bf16 = jnp.bfloat16


def gelu_slope(t):
    c = 0.7978845608028654
    sq = t * t
    th = jnp.tanh(c * t * (1.0 + 0.044715 * sq))
    return 0.5 * (1.0 + th) + 0.5 * t * (1.0 - th * th) * (c * (1.0 + 3 * 0.044715 * sq))


def pair_kernel(
    x_hbm, cot_hbm, p_ref,
    out_ref, g_ref,
    xb, xt, cb, w, g, rah, raf, rbh, rbf, pws, pwr, gps, gpr, bks, bkr, tmp, acc,
    loc_sem, ag_send, ag_recv, rs_send, rs_recv, pw_send, pw_recv,
    x_send, x_recv, cot_send, cot_recv, bk_send, bk_recv, gp_send, gp_recv,
):
    tok, width = x_hbm.shape
    rows, ffw = p_ref.shape
    half_cols = ffw // 2
    n_chunks = half_cols // CHUNK
    block = 2 * rows
    pad_rows = pwr.shape[2]
    cut = (block // 16 + 1) // 2 * 16
    n_x = x_send.shape[0]
    x_rows = tok // n_x
    n_bk = bk_send.shape[0]
    bk_rows = tok // (n_bk // 2)
    bk_cols = width // 2
    scale = width ** (-0.5)

    f = lax.axis_index("fsdp")
    yh = lax.rem(f, 2)
    x = lax.rem(lax.div(f, 2), 4)
    z = lax.div(f, 8)

    def device(zz, xx, yy):
        return {"fsdp": zz * 8 + xx * 2 + yy}

    peer = device(z, x, 1 - yh)
    place = {"x": x, "z": z}
    after = {a: lax.rem(place[a] + 1, 4) for a in place}
    before = {a: lax.rem(place[a] + 3, 4) for a in place}
    across = {a: lax.rem(place[a] + 2, 4) for a in place}
    right = {"x": device(z, after["x"], yh), "z": device(after["z"], x, yh)}
    left = {"x": device(z, before["x"], yh), "z": device(before["z"], x, yh)}
    first_axis = ("x", "z")
    second_axis = ("z", "x")
    my_base = yh * half_cols
    peer_base = (1 - yh) * half_cols

    def seg2(ref, u, p, i):
        return ref.at[u, i] if p == 0 else ref.at[u, :, i]

    def half2(ref, u, p, i, h):
        part = pl.ds(2 * h, 2)
        return ref.at[u, i, part] if p == 0 else ref.at[u, part, i]

    def seg1(ref, u, p, i):
        return ref.at[u, z, i] if p == 0 else ref.at[u, i, x]

    def half1(ref, u, p, i, h):
        part = pl.ds(0, cut) if h == 0 else pl.ds(cut, block - cut)
        return ref.at[u, z, i, part] if p == 0 else ref.at[u, i, x, part]

    def remote(src, dst, send, recv, to):
        return pltpu.make_async_remote_copy(
            src_ref=src, dst_ref=dst, send_sem=send, recv_sem=recv, device_id=to, device_id_type=MESH
        )

    def gather_copy(u, p, k):
        a, b = first_axis[p], second_axis[p]
        part = (
            lambda: seg1(w, u, p, place[a]),
            lambda: seg1(w, u, p, place[a]),
            lambda: half1(w, u, p, before[a], 0),
            lambda: half1(w, u, p, after[a], 1),
            lambda: seg2(w, u, p, place[b]),
            lambda: seg2(w, u, p, place[b]),
            lambda: half2(w, u, p, before[b], 0),
            lambda: half2(w, u, p, after[b], 1),
        )[k]()
        to = (right if k % 2 == 0 else left)[a if k < 4 else b]
        return remote(part, part, ag_send.at[u, k], ag_recv.at[u, k], to)

    def scatter_copy(u, p, k):
        a, b = first_axis[p], second_axis[p]
        src, dst = (
            lambda: (half2(g, u, p, across[b], 0), rah.at[u, 0]),
            lambda: (half2(g, u, p, across[b], 1), rah.at[u, 1]),
            lambda: (seg2(g, u, p, after[b]), raf.at[u, 0]),
            lambda: (seg2(g, u, p, before[b]), raf.at[u, 1]),
            lambda: (half1(g, u, p, across[a], 0), rbh.at[u, pl.ds(0, cut)]),
            lambda: (half1(g, u, p, across[a], 1), rbh.at[u, pl.ds(cut, block - cut)]),
            lambda: (seg1(g, u, p, after[a]), rbf.at[u, 0]),
            lambda: (seg1(g, u, p, before[a]), rbf.at[u, 1]),
        )[k]()
        to = (right if k % 2 == 0 else left)[b if k < 4 else a]
        return remote(src, dst, rs_send.at[u, k], rs_recv.at[u, k], to)

    def pw_copy(c):
        return remote(pws.at[c], pwr.at[c], pw_send.at[c], pw_recv.at[c], peer)

    def x_copy(i):
        return remote(
            x_hbm.at[pl.ds(i * x_rows, x_rows)], xb.at[pl.ds(tok + i * x_rows, x_rows)],
            x_send.at[i], x_recv.at[i], peer,
        )

    def cot_copy(c):
        cols = pl.ds(pl.multiple_of(peer_base + c * CHUNK, CHUNK), CHUNK)
        return remote(
            cot_hbm.at[:, cols], cb.at[c, pl.ds(tok, tok)], cot_send.at[c], cot_recv.at[c], peer
        )

    def bk_copy(i):
        return remote(bks.at[i], bkr.at[i], bk_send.at[i], bk_recv.at[i], peer)

    def gp_copy(u):
        return remote(gps.at[u], gpr.at[u], gp_send.at[u], gp_recv.at[u], peer)

    def own_x():
        return pltpu.make_async_copy(x_hbm, xb.at[pl.ds(0, tok)], loc_sem.at[n_chunks])

    def own_cot(c):
        cols = pl.ds(pl.multiple_of(my_base + c * CHUNK, CHUNK), CHUNK)
        return pltpu.make_async_copy(cot_hbm.at[:, cols], cb.at[c, pl.ds(0, tok)], loc_sem.at[c])

    def each(count, step):
        def run(i, carry):
            step(i)
            return carry
        lax.fori_loop(0, count, run, 0)

    def ranged(t, lag, step):
        @pl.when((t >= lag) & (t < lag + n_chunks))
        def _():
            step(t - lag)

    def both(step):
        def run(c):
            for p in range(2):
                step(2 * c + p, p)
        return run

    own_x().start()
    each(n_chunks, lambda c: own_cot(c).start())

    def prepare(c):
        for h in range(2):
            cols = pl.ds(pl.multiple_of(peer_base + c * CHUNK + h * LANES, LANES), LANES)
            part = jnp.concatenate([p_ref[:, cols], jnp.zeros((pad_rows - rows, LANES), f32)], axis=0)
            pws[c, h] = part.astype(bf16)

    each(n_chunks, prepare)

    barrier = pltpu.get_barrier_semaphore()
    partners = (peer, right["x"], left["x"], right["z"], left["z"])
    for partner in partners:
        pl.semaphore_signal(barrier, inc=1, device_id=partner, device_id_type=MESH)
    pl.semaphore_wait(barrier, len(partners))

    each(n_chunks, lambda c: pw_copy(c).start())
    each(n_x, lambda i: x_copy(i).start())

    def transpose_rows(start, count):
        def step(k):
            cols = pl.ds(pl.multiple_of(k * LANES, LANES), LANES)
            part = xb[pl.ds(start, count), cols].astype(f32)
            xt[cols, pl.ds(start, count)] = part.T.astype(bf16)
        each(width // LANES, step)

    def chunk_weights(c):
        return jnp.concatenate(
            [w[2 * c].reshape(width, LANES), w[2 * c + 1].reshape(width, LANES)], axis=1
        )

    def hidden(c, start):
        at = pl.ds(start, tok)
        pre = jnp.dot(xb[at, :], chunk_weights(c), preferred_element_type=f32) * scale
        cot = cb[c, at, :].astype(f32)
        cb[c, at, :] = (gelu_slope(pre) * cot * scale).astype(bf16)

    def gather_own(c):
        pw_copy(c).wait_recv()
        for h in range(2):
            cols = pl.ds(pl.multiple_of(my_base + c * CHUNK + h * LANES, LANES), LANES)
            tmp[pl.ds(pl.multiple_of(yh * rows, 8), rows), :] = p_ref[:, cols]
            tmp[pl.ds(pl.multiple_of((1 - yh) * rows, 8), rows), :] = pwr[c, h].astype(f32)[:rows]
            w[2 * c + h, z, x] = tmp[...].astype(bf16)
            gather_copy(2 * c + h, h, 0).start()
            gather_copy(2 * c + h, h, 1).start()

    def gather_forward(k):
        def step(u, p):
            gather_copy(u, p, k).wait_recv()
            gather_copy(u, p, k + 2).start()
            gather_copy(u, p, k + 1).wait_recv()
            gather_copy(u, p, k + 3).start()
        return both(step)

    @both
    def gather_second(u, p):
        gather_copy(u, p, 2).wait_recv()
        gather_copy(u, p, 3).wait_recv()
        gather_copy(u, p, 4).start()
        gather_copy(u, p, 5).start()

    @both
    def gather_end(u, p):
        gather_copy(u, p, 6).wait_recv()
        gather_copy(u, p, 7).wait_recv()

    def own_hidden(c):
        gather_end(c)
        own_cot(c).wait()
        hidden(c, 0)

    def gather_tick(t):
        ranged(t, 0, gather_own)
        ranged(t, 1, gather_forward(0))
        ranged(t, 2, gather_second)
        ranged(t, 3, gather_forward(4))

        @pl.when(t == 2)
        def _():
            own_x().wait()
            transpose_rows(0, tok)

        @pl.when(t == n_chunks)
        def _():
            cot_copy(0).start()
            cot_copy(1).start()

        ranged(t, 4, own_hidden)

    each(n_chunks + 4, gather_tick)

    for i in range(n_x):
        x_copy(i).wait_recv()
        transpose_rows(tok + i * x_rows, x_rows)

    def add_into(ref, other):
        ref[...] = (ref[...].astype(f32) + other[...].astype(f32)).astype(bf16)

    def work(c):
        cot_copy(c).wait_recv()

        @pl.when(c + 2 < n_chunks)
        def _():
            cot_copy(c + 2).start()

        hidden(c, tok)

        def block_grad(i):
            at = pl.ds(pl.multiple_of(i * 4 * block, LANES // 2), 4 * block)
            term = jnp.dot(xt[at, :], cb[c], preferred_element_type=f32).astype(bf16)
            g[2 * c, i] = term[:, :LANES].reshape(4, block, LANES)
            g[2 * c + 1, i] = term[:, LANES:].reshape(4, block, LANES)

        each(4, block_grad)
        for p in range(2):
            scatter_copy(2 * c + p, p, 0).start()
            scatter_copy(2 * c + p, p, 1).start()

    @both
    def scatter_second(u, p):
        b = second_axis[p]
        scatter_copy(u, p, 0).wait_recv()
        add_into(half2(g, u, p, after[b], 0), rah.at[u, 0])
        scatter_copy(u, p, 2).start()
        scatter_copy(u, p, 1).wait_recv()
        add_into(half2(g, u, p, before[b], 1), rah.at[u, 1])
        scatter_copy(u, p, 3).start()

    @both
    def scatter_third(u, p):
        b = second_axis[p]
        scatter_copy(u, p, 2).wait_recv()
        scatter_copy(u, p, 3).wait_recv()
        mine = seg2(g, u, p, place[b])
        mine[...] = (
            mine[...].astype(f32) + raf[u, 0].astype(f32) + raf[u, 1].astype(f32)
        ).astype(bf16)
        scatter_copy(u, p, 4).start()
        scatter_copy(u, p, 5).start()

    @both
    def scatter_fourth(u, p):
        a = first_axis[p]
        scatter_copy(u, p, 4).wait_recv()
        add_into(half1(g, u, p, after[a], 0), rbh.at[u, pl.ds(0, cut)])
        scatter_copy(u, p, 6).start()
        scatter_copy(u, p, 5).wait_recv()
        add_into(half1(g, u, p, before[a], 1), rbh.at[u, pl.ds(cut, block - cut)])
        scatter_copy(u, p, 7).start()

    @both
    def scatter_end(u, p):
        a = first_axis[p]
        scatter_copy(u, p, 6).wait_recv()
        scatter_copy(u, p, 7).wait_recv()
        mine = seg1(g, u, p, place[a])
        tmp[...] = mine[...].astype(f32) + rbf[u, 0].astype(f32) + rbf[u, 1].astype(f32)
        theirs = tmp[pl.ds(pl.multiple_of((1 - yh) * rows, 8), rows), :]
        theirs = jnp.concatenate([theirs, jnp.zeros((pad_rows - rows, LANES), f32)], axis=0)
        gps[u] = theirs.astype(bf16)
        gp_copy(u).start()
        cols = pl.ds(pl.multiple_of(my_base + u * LANES, LANES), LANES)
        g_ref[:, cols] = tmp[pl.ds(pl.multiple_of(yh * rows, 8), rows), :]

    def back_tile(i, start):
        m, n = lax.div(i, 2), lax.rem(i, 2)
        at = pl.ds(pl.multiple_of(start + m * bk_rows, 16), bk_rows)
        acc[...] = jnp.zeros_like(acc)

        def step(c):
            part = jnp.concatenate(
                [w[2 * c + h, pl.ds(2 * n, 2)].reshape(bk_cols, LANES) for h in range(2)], axis=1
            )
            acc[...] += lax.dot_general(
                cb[c, at, :], part, (((1,), (1,)), ((), ())), preferred_element_type=f32
            )

        each(n_chunks, step)

    def send_back(i):
        back_tile(i, tok)
        bks[i] = acc[...].astype(bf16)
        bk_copy(i).start()

    def work_tick(t):
        ranged(t, 0, work)

        @pl.when((t >= n_chunks) & (t < n_chunks + n_bk // 2))
        def _():
            send_back(2 * (t - n_chunks))
            send_back(2 * (t - n_chunks) + 1)

        ranged(t, 2, scatter_second)
        ranged(t, 3, scatter_third)
        ranged(t, 4, scatter_fourth)
        ranged(t, 5, scatter_end)

    each(n_chunks + 5, work_tick)

    def finish_back(i):
        back_tile(i, 0)
        bk_copy(i).wait_recv()
        m, n = lax.div(i, 2), lax.rem(i, 2)
        at = pl.ds(pl.multiple_of(m * bk_rows, 16), bk_rows)
        cols = pl.ds(pl.multiple_of(n * bk_cols, LANES), bk_cols)
        out_ref[at, cols] = (acc[...] + bkr[i].astype(f32)).astype(bf16)

    each(n_bk, finish_back)

    def finish_grad(u):
        gp_copy(u).wait_recv()
        cols = pl.ds(pl.multiple_of(peer_base + u * LANES, LANES), LANES)
        g_ref[:, cols] = gpr[u].astype(f32)[:rows]

    each(2 * n_chunks, finish_grad)

    def settle(c):
        pw_copy(c).wait_send()
        cot_copy(c).wait_send()
        for p in range(2):
            u = 2 * c + p
            gp_copy(u).wait_send()
            for k in range(8):
                gather_copy(u, p, k).wait_send()
                scatter_copy(u, p, k).wait_send()

    each(n_chunks, settle)
    each(n_x, lambda i: x_copy(i).wait_send())
    each(n_bk, lambda i: bk_copy(i).wait_send())


def projection(acts, cot, weights):
    tok, width = acts.shape
    rows, ffw = weights.shape
    units = ffw // 2 // LANES
    chunks = units // 2
    block = 2 * rows
    pad_rows = (rows + 15) // 16 * 16
    n_x, n_bk = 3, 6
    dma = pltpu.SemaphoreType.DMA
    vmem = pltpu.VMEM
    return pl.pallas_call(
        pair_kernel,
        out_shape=(
            jax.ShapeDtypeStruct((tok, width), bf16),
            jax.ShapeDtypeStruct((rows, ffw), f32),
        ),
        in_specs=[
            pl.BlockSpec(memory_space=pl.ANY),
            pl.BlockSpec(memory_space=pl.ANY),
            pl.BlockSpec(memory_space=pltpu.VMEM),
        ],
        out_specs=(
            pl.BlockSpec(memory_space=pltpu.VMEM),
            pl.BlockSpec(memory_space=pltpu.VMEM),
        ),
        scratch_shapes=[
            vmem((2 * tok, width), bf16),
            vmem((width, 2 * tok), bf16),
            vmem((chunks, 2 * tok, CHUNK), bf16),
            vmem((units, 4, 4, block, LANES), bf16),
            vmem((units, 4, 4, block, LANES), bf16),
            vmem((units, 2, 2, block, LANES), bf16),
            vmem((units, 2, 4, block, LANES), bf16),
            vmem((units, block, LANES), bf16),
            vmem((units, 2, block, LANES), bf16),
            vmem((chunks, 2, pad_rows, LANES), bf16),
            vmem((chunks, 2, pad_rows, LANES), bf16),
            vmem((units, pad_rows, LANES), bf16),
            vmem((units, pad_rows, LANES), bf16),
            vmem((n_bk, tok // (n_bk // 2), width // 2), bf16),
            vmem((n_bk, tok // (n_bk // 2), width // 2), bf16),
            vmem((block, LANES), f32),
            vmem((tok // (n_bk // 2), width // 2), f32),
            dma((chunks + 1,)),
            dma((units, 8)), dma((units, 8)),
            dma((units, 8)), dma((units, 8)),
            dma((chunks,)), dma((chunks,)),
            dma((n_x,)), dma((n_x,)),
            dma((chunks,)), dma((chunks,)),
            dma((n_bk,)), dma((n_bk,)),
            dma((units,)), dma((units,)),
        ],
        compiler_params=pltpu.CompilerParams(
            collective_id=1, has_side_effects=True, vmem_limit_bytes=60 * 2**20
        ),
        cost_estimate=pl.CostEstimate(
            flops=6 * tok * width * ffw, bytes_accessed=16 * tok * width, transcendentals=tok * ffw
        ),
        name="pair_projection",
    )(acts, cot, weights)


def body(inputs, cotangent, params, first_moment, second_moment, snapshot, momentum, fragment):
    weights = params[0]
    frag = snapshot.shape[1]
    start_col = fragment[0] * frag
    local = lax.dynamic_slice_in_dim(weights, start_col, frag, 1)
    total = lax.psum((snapshot - local).astype(bf16), "rep").astype(f32)
    input_grad, grad = projection(inputs[0], cotangent[0], weights)
    outer_grad = total / lax.axis_size("rep")
    new_momentum = outer_mu * momentum + outer_grad
    new_snapshot = snapshot - outer_rate * (outer_grad + outer_mu * new_momentum)
    first = beta_one * first_moment[0] + (1.0 - beta_one) * grad
    second = beta_two * second_moment[0] + (1.0 - beta_two) * grad * grad
    stepped = weights - inner_rate * (first / (jnp.sqrt(second) + adam_eps) + decay_rate * weights)
    frag_part = lax.dynamic_slice_in_dim(stepped, start_col, frag, 1)
    merged = mix_rate * new_snapshot + (1.0 - mix_rate) * frag_part
    stepped = lax.dynamic_update_slice_in_dim(stepped, merged, start_col, 1)
    return (stepped[None], first[None], second[None], input_grad[None], new_momentum, new_snapshot)


def solution(mesh):
    return jax.shard_map(
        body,
        mesh=mesh,
        in_specs=(
            P("rep", "fsdp", None),
            P("rep", "fsdp", None),
            P("rep", "fsdp", None),
            P("rep", "fsdp", None),
            P("rep", "fsdp", None),
            P("fsdp", None),
            P("fsdp", None),
            P(),
        ),
        out_specs=(
            P("rep", "fsdp", None),
            P("rep", "fsdp", None),
            P("rep", "fsdp", None),
            P("rep", "fsdp", None),
            P("fsdp", None),
            P("fsdp", None),
        ),
        check_vma=False,
    )
```

time: 563 us -> 202 us (0.36)
  waiting for transfers between devices: 456 us -> 0.02 us
  Pallas kernels: 0 us -> 176 us
  matrix products: 47.2 us -> 0 us
  local copies, waits for them, and re-layouts: 33.5 us -> 2.38 us
    reduce_scatter x1 -> x0, waiting for transfers between devices: 269 us -> none  [body(): lax.psum_scatter(lax.dot_general(acts, hidden_cot, (((0,), (0,)), ((), ()...]
    all_gather x1 -> x0, waiting for transfers between devices: 187 us -> none  [body(): whole = lax.all_gather(shard_low, 'fsdp', axis=0, tiled=True)]
    pallas_call x0 -> x1, Pallas kernels: none -> 176 us  [projection(): pl.pallas_call(pair_kernel, out_shape=(jax.ShapeDtypeStruct((tok, width),...]
    dot_general x3 -> x0, matrix products: 47.2 us -> none  [the longest x1 17.2 us: body(): pre = jnp.dot(acts, whole, preferred_element_type=jnp.float32) * scale]
    unnamed x18 -> x8, local copies, waits for them, and re-layouts: 33.5 us -> 2.38 us
  transfers between devices with their start and end apart: 3 -> 1, of which waited for: 2 -> 0; matrix products, arithmetic and copies ran while one was open for 4% -> 3% of each run, Pallas kernels for 0% -> 87%
where the time goes in v1:
time: 202 us
  Pallas kernels  176 us (87%)
  between operations  14.7 us (7%)
  other arithmetic  8.5 us (4%)
  local copies, waits for them, and re-layouts  2.38 us (1%)
    pallas_call x1, Pallas kernels, projection(): pl.pallas_call(pair_kernel, out_shape=(jax.ShapeDtypeStruct((tok, width),...  176 us
    broadcast_in_dim x1, other arithmetic, body(): second[None]  4.53 us
  transfers between devices with their start and end apart: 1, of which 0 were waited for; matrix products, arithmetic and copies ran while one was open for 3% of the time, Pallas kernels for 87%

profile of v1, /device:TPU:0, one launch (start us, length us, event | category | flops | bytes accessed | tf_op | source)
XLA Modules:
  0.0 202.1 jit_solution(3074116523251720821)
XLA Ops:
  7.2 0.0 all-reduce.2.cloned.1.call-start
  7.9 1.8 fusion.3
  9.6 0.0 all-reduce.2.cloned.1.call-update
  9.7 0.0 copy-start
  9.7 176.4 %pair_projection.1 = (bf16[384,2304]{1,0:T(8,128)(2,1)}, f32[72,4608]{1,0:T(8,128)}) custom-call(bf16[384,2304]{1,0:T(8,128)(2,1)} %bitcast.34, bf16[384,4608]{1,0:T(8,128)(2,1)} %bitcast.33, f32[72,4608]{1,0:T(8,128)} %bitcast.31), custom_call_target="tpu_custom_call" | custom-call | flops 24461180928 | bytes 14155776 | tf_op jit(solution)/shard_map/pair_projection/pallas_call | solution.py:411
  186.1 0.0 copy-done
  186.1 4.5 %fusion.2 = (f32[1,72,4608]{2,1,0:T(8,128)}, f32[72,4608]{1,0:T(8,128)S(1)}, f32[1,72,4608]{2,1,0:T(8,128)}) fusion(f32[72,4608]{1,0:T(8,128)} %get-tuple-element.8, f32[1,72,4608]{2,1,0:T(8,128)} %param.12, f32[1,72,4608]{2,1,0:T(8,128)} %param.11, f32[1,72,4608]{2,1,0:T(8,128)S(1)} %copy-done), kind=kLoop, calls=%fused_computation.5 | loop fusion | flops 4313088 | bytes 9289728 | tf_op jit(solution)/shard_map/broadcast_in_dim | solution.py:479
  190.6 0.0 copy-start.2
  190.6 1.1 copy.15
  191.7 0.0 copy-start.1
  191.7 0.0 all-reduce.2.cloned.1.call-done
  191.7 0.1 copy-done.2
  191.8 2.2 %bitcast_dynamic-update-slice_fusion = (f32[1,72,4608]{2,1,0:T(8,128)}, f32[72,1152]{1,0:T(8,128)}, f32[72,1152]{1,0:T(8,128)}) fusion(f32[1,72,4608]{2,1,0:T(8,128)} %copy.15, s32[]{:T(128)S(6)} %select_n.2, f32[72,4608]{1,0:T(8,128)S(1)} %get-tuple-element.14, f32[72,1152]{1,0:T(8,128)S(1)} %copy-done.2, bf16[72,1152]{1,0:T(8,128)(2,1)} %all-reduce.2.cloned.1.call-done, ...), kind=kLoop, calls=%fused_computation.6 | loop fusion | flops 829440 | bytes 2156548 | tf_op jit(solution)/shard_map/dynamic_update_slice | solution.py:478
  194.0 0.0 copy-done.1
  194.0 1.2 copy.17
Async XLA Ops:
  7.2 184.5 %all-reduce.2.cloned.1.call-start = ((), (), s32[]{:S(2)}) async-start(), calls=%async_computation | async-start | bytes 331776 | tf_op jit(solution)/shard_map/psum | solution.py:468
  9.7 176.4 %copy-start = (f32[1,72,4608]{2,1,0:T(8,128)S(1)}, f32[1,72,4608]{2,1,0:T(8,128)}, u32[]{:S(2)}) copy-start(f32[1,72,4608]{2,1,0:T(8,128)} %param.10) | copy-start | bytes 3981316
  190.6 1.2 copy-start.2
  191.7 2.3 %copy-start.1 = (bf16[384,2304]{1,0:T(8,128)(2,1)S(1)}, bf16[384,2304]{1,0:T(8,128)(2,1)}, u32[]{:S(2)}) copy-start(bf16[384,2304]{1,0:T(8,128)(2,1)} %get-tuple-element.9) | copy-start | bytes 5308420
Sparse Core Ops, SparseCore 0:
  11.1 39.2 all-reduce.1

commit v2 on v1

--- a/solution.py
+++ b/solution.py
@@ -33,7 +33,7 @@
 def pair_kernel(
     x_hbm, cot_hbm, p_ref,
     out_ref, g_ref,
-    xb, xt, cb, w, g, rah, raf, rbh, rbf, pws, pwr, gps, gpr, bks, bkr, tmp, acc,
+    xb, cb, w, g, rah, raf, rbh, rbf, pws, pwr, gps, gpr, bks, bkr, tmp, acc,
     loc_sem, ag_send, ag_recv, rs_send, rs_recv, pw_send, pw_recv,
     x_send, x_recv, cot_send, cot_recv, bk_send, bk_recv, gp_send, gp_recv,
 ):
@@ -50,6 +50,9 @@
     bk_rows = tok // (n_bk // 2)
     bk_cols = width // 2
     scale = width ** (-0.5)
+    ahead = 4
+    work_lag = 10
+    done = work_lag + n_chunks
 
     f = lax.axis_index("fsdp")
     yh = lax.rem(f, 2)
@@ -84,6 +87,9 @@
     def half1(ref, u, p, i, h):
         part = pl.ds(0, cut) if h == 0 else pl.ds(cut, block - cut)
         return ref.at[u, z, i, part] if p == 0 else ref.at[u, i, x, part]
+
+    def chunk_cols(c):
+        return pl.ds(pl.multiple_of(c * CHUNK, CHUNK), CHUNK)
 
     def remote(src, dst, send, recv, to):
         return pltpu.make_async_remote_copy(
@@ -132,7 +138,8 @@
     def cot_copy(c):
         cols = pl.ds(pl.multiple_of(peer_base + c * CHUNK, CHUNK), CHUNK)
         return remote(
-            cot_hbm.at[:, cols], cb.at[c, pl.ds(tok, tok)], cot_send.at[c], cot_recv.at[c], peer
+            cot_hbm.at[:, cols], cb.at[pl.ds(tok, tok), chunk_cols(c)],
+            cot_send.at[c], cot_recv.at[c], peer,
         )
 
     def bk_copy(i):
@@ -146,7 +153,9 @@
 
     def own_cot(c):
         cols = pl.ds(pl.multiple_of(my_base + c * CHUNK, CHUNK), CHUNK)
-        return pltpu.make_async_copy(cot_hbm.at[:, cols], cb.at[c, pl.ds(0, tok)], loc_sem.at[c])
+        return pltpu.make_async_copy(
+            cot_hbm.at[:, cols], cb.at[pl.ds(0, tok), chunk_cols(c)], loc_sem.at[c]
+        )
 
     def each(count, step):
         def run(i, carry):
@@ -185,13 +194,6 @@
     each(n_chunks, lambda c: pw_copy(c).start())
     each(n_x, lambda i: x_copy(i).start())
 
-    def transpose_rows(start, count):
-        def step(k):
-            cols = pl.ds(pl.multiple_of(k * LANES, LANES), LANES)
-            part = xb[pl.ds(start, count), cols].astype(f32)
-            xt[cols, pl.ds(start, count)] = part.T.astype(bf16)
-        each(width // LANES, step)
-
     def chunk_weights(c):
         return jnp.concatenate(
             [w[2 * c].reshape(width, LANES), w[2 * c + 1].reshape(width, LANES)], axis=1
@@ -200,8 +202,8 @@
     def hidden(c, start):
         at = pl.ds(start, tok)
         pre = jnp.dot(xb[at, :], chunk_weights(c), preferred_element_type=f32) * scale
-        cot = cb[c, at, :].astype(f32)
-        cb[c, at, :] = (gelu_slope(pre) * cot * scale).astype(bf16)
+        cot = cb[at, chunk_cols(c)].astype(f32)
+        cb[at, chunk_cols(c)] = (gelu_slope(pre) * cot * scale).astype(bf16)
 
     def gather_own(c):
         pw_copy(c).wait_recv()
@@ -238,49 +240,22 @@
         own_cot(c).wait()
         hidden(c, 0)
 
-    def gather_tick(t):
-        ranged(t, 0, gather_own)
-        ranged(t, 1, gather_forward(0))
-        ranged(t, 2, gather_second)
-        ranged(t, 3, gather_forward(4))
-
-        @pl.when(t == 2)
-        def _():
-            own_x().wait()
-            transpose_rows(0, tok)
-
-        @pl.when(t == n_chunks)
-        def _():
-            cot_copy(0).start()
-            cot_copy(1).start()
-
-        ranged(t, 4, own_hidden)
-
-    each(n_chunks + 4, gather_tick)
-
-    for i in range(n_x):
-        x_copy(i).wait_recv()
-        transpose_rows(tok + i * x_rows, x_rows)
-
     def add_into(ref, other):
         ref[...] = (ref[...].astype(f32) + other[...].astype(f32)).astype(bf16)
 
     def work(c):
         cot_copy(c).wait_recv()
 
-        @pl.when(c + 2 < n_chunks)
-        def _():
-            cot_copy(c + 2).start()
+        @pl.when(c + ahead < n_chunks)
+        def _():
+            cot_copy(c + ahead).start()
 
         hidden(c, tok)
-
-        def block_grad(i):
-            at = pl.ds(pl.multiple_of(i * 4 * block, LANES // 2), 4 * block)
-            term = jnp.dot(xt[at, :], cb[c], preferred_element_type=f32).astype(bf16)
-            g[2 * c, i] = term[:, :LANES].reshape(4, block, LANES)
-            g[2 * c + 1, i] = term[:, LANES:].reshape(4, block, LANES)
-
-        each(4, block_grad)
+        term = lax.dot_general(
+            xb[...], cb[:, chunk_cols(c)], (((0,), (0,)), ((), ())), preferred_element_type=f32
+        ).astype(bf16)
+        for h in range(2):
+            g[2 * c + h] = term[:, h * LANES : (h + 1) * LANES].reshape(4, 4, block, LANES)
         for p in range(2):
             scatter_copy(2 * c + p, p, 0).start()
             scatter_copy(2 * c + p, p, 1).start()
@@ -331,48 +306,69 @@
         cols = pl.ds(pl.multiple_of(my_base + u * LANES, LANES), LANES)
         g_ref[:, cols] = tmp[pl.ds(pl.multiple_of(yh * rows, 8), rows), :]
 
-    def back_tile(i, start):
-        m, n = lax.div(i, 2), lax.rem(i, 2)
-        at = pl.ds(pl.multiple_of(start + m * bk_rows, 16), bk_rows)
-        acc[...] = jnp.zeros_like(acc)
-
-        def step(c):
-            part = jnp.concatenate(
-                [w[2 * c + h, pl.ds(2 * n, 2)].reshape(bk_cols, LANES) for h in range(2)], axis=1
-            )
-            acc[...] += lax.dot_general(
-                cb[c, at, :], part, (((1,), (1,)), ((), ())), preferred_element_type=f32
-            )
-
-        each(n_chunks, step)
-
-    def send_back(i):
-        back_tile(i, tok)
-        bks[i] = acc[...].astype(bf16)
-        bk_copy(i).start()
-
-    def work_tick(t):
-        ranged(t, 0, work)
-
-        @pl.when((t >= n_chunks) & (t < n_chunks + n_bk // 2))
-        def _():
-            send_back(2 * (t - n_chunks))
-            send_back(2 * (t - n_chunks) + 1)
-
-        ranged(t, 2, scatter_second)
-        ranged(t, 3, scatter_third)
-        ranged(t, 4, scatter_fourth)
-        ranged(t, 5, scatter_end)
-
-    each(n_chunks + 5, work_tick)
+    def back_half(n, start):
+        part = jnp.concatenate(
+            [w[u, pl.ds(2 * n, 2)].reshape(bk_cols, LANES) for u in range(2 * n_chunks)], axis=1
+        )
+        return lax.dot_general(
+            cb[pl.ds(start, tok), :], part, (((1,), (1,)), ((), ())), preferred_element_type=f32
+        )
+
+    def send_back(n):
+        term = back_half(n, tok).astype(bf16)
+        for m in range(n_bk // 2):
+            i = n * (n_bk // 2) + m
+            bks[i] = term[m * bk_rows : (m + 1) * bk_rows]
+            bk_copy(i).start()
+
+    def keep_back(n):
+        acc[n] = back_half(n, 0)
+
+    def tick(t):
+        ranged(t, 0, gather_own)
+        ranged(t, 1, gather_forward(0))
+        ranged(t, 2, gather_second)
+        ranged(t, 3, gather_forward(4))
+
+        @pl.when(t == 4)
+        def _():
+            own_x().wait()
+
+        ranged(t, 4, own_hidden)
+
+        @pl.when(t == 7)
+        def _():
+            for c in range(ahead):
+                cot_copy(c).start()
+
+        @pl.when(t == work_lag)
+        def _():
+            for i in range(n_x):
+                x_copy(i).wait_recv()
+
+        ranged(t, work_lag, work)
+
+        @pl.when((t >= done) & (t < done + 2))
+        def _():
+            send_back(t - done)
+
+        @pl.when((t >= done + 2) & (t < done + 4))
+        def _():
+            keep_back(t - done - 2)
+
+        ranged(t, work_lag + 3, scatter_second)
+        ranged(t, work_lag + 6, scatter_third)
+        ranged(t, work_lag + 8, scatter_fourth)
+        ranged(t, work_lag + 9, scatter_end)
+
+    each(n_chunks + work_lag + 9, tick)
 
     def finish_back(i):
-        back_tile(i, 0)
         bk_copy(i).wait_recv()
-        m, n = lax.div(i, 2), lax.rem(i, 2)
+        n, m = lax.div(i, n_bk // 2), lax.rem(i, n_bk // 2)
         at = pl.ds(pl.multiple_of(m * bk_rows, 16), bk_rows)
         cols = pl.ds(pl.multiple_of(n * bk_cols, LANES), bk_cols)
-        out_ref[at, cols] = (acc[...] + bkr[i].astype(f32)).astype(bf16)
+        out_ref[at, cols] = (acc[n, at, :] + bkr[i].astype(f32)).astype(bf16)
 
     each(n_bk, finish_back)
 
@@ -425,8 +421,7 @@
         ),
         scratch_shapes=[
             vmem((2 * tok, width), bf16),
-            vmem((width, 2 * tok), bf16),
-            vmem((chunks, 2 * tok, CHUNK), bf16),
+            vmem((2 * tok, ffw // 2), bf16),
             vmem((units, 4, 4, block, LANES), bf16),
             vmem((units, 4, 4, block, LANES), bf16),
             vmem((units, 2, 2, block, LANES), bf16),
@@ -440,7 +435,7 @@
             vmem((n_bk, tok // (n_bk // 2), width // 2), bf16),
             vmem((n_bk, tok // (n_bk // 2), width // 2), bf16),
             vmem((block, LANES), f32),
-            vmem((tok // (n_bk // 2), width // 2), f32),
+            vmem((2, tok, width // 2), f32),
             dma((chunks + 1,)),
             dma((units, 8)), dma((units, 8)),
             dma((units, 8)), dma((units, 8)),

time: 202 us -> 183 us (0.906)
  Pallas kernels: 176 us -> 157 us
    pallas_call x1, Pallas kernels: 176 us -> 157 us  [projection(): pl.pallas_call(pair_kernel, out_shape=(jax.ShapeDtypeStruct((tok, width),...]
  transfers between devices with their start and end apart: 1 -> 1, of which waited for: 0 -> 0; matrix products, arithmetic and copies ran while one was open for 3% -> 3% of each run, Pallas kernels for 87% -> 86%
where the time goes in v2:
time: 183 us
  Pallas kernels  157 us (86%)
  between operations  14.7 us (8%)
  other arithmetic  8.5 us (5%)
  local copies, waits for them, and re-layouts  2.38 us (1%)
    pallas_call x1, Pallas kernels, projection(): pl.pallas_call(pair_kernel, out_shape=(jax.ShapeDtypeStruct((tok, width),...  157 us
    broadcast_in_dim x1, other arithmetic, body(): second[None]  4.53 us
  transfers between devices with their start and end apart: 1, of which 0 were waited for; matrix products, arithmetic and copies ran while one was open for 3% of the time, Pallas kernels for 86%

profile of v2, /device:TPU:0, one launch (start us, length us, event | category | flops | bytes accessed | tf_op | source)
XLA Modules:
  0.0 183.0 jit_solution(9355875515457332127)
XLA Ops:
  7.2 0.0 all-reduce.2.cloned.1.call-start
  7.9 1.8 fusion.3
  9.6 0.0 all-reduce.2.cloned.1.call-update
  9.7 0.0 copy-start
  9.7 157.3 %pair_projection.1 = (bf16[384,2304]{1,0:T(8,128)(2,1)}, f32[72,4608]{1,0:T(8,128)}) custom-call(bf16[384,2304]{1,0:T(8,128)(2,1)} %bitcast.34, bf16[384,4608]{1,0:T(8,128)(2,1)} %bitcast.33, f32[72,4608]{1,0:T(8,128)} %bitcast.31), custom_call_target="tpu_custom_call" | custom-call | flops 24461180928 | bytes 14155776 | tf_op jit(solution)/shard_map/pair_projection/pallas_call | solution.py:407
  167.0 0.0 copy-done
  167.0 4.5 %fusion.2 = (f32[1,72,4608]{2,1,0:T(8,128)}, f32[72,4608]{1,0:T(8,128)S(1)}, f32[1,72,4608]{2,1,0:T(8,128)}) fusion(f32[72,4608]{1,0:T(8,128)} %get-tuple-element.8, f32[1,72,4608]{2,1,0:T(8,128)} %param.12, f32[1,72,4608]{2,1,0:T(8,128)} %param.11, f32[1,72,4608]{2,1,0:T(8,128)S(1)} %copy-done), kind=kLoop, calls=%fused_computation.5 | loop fusion | flops 4313088 | bytes 9289728 | tf_op jit(solution)/shard_map/broadcast_in_dim | solution.py:474
  171.6 0.0 copy-start.2
  171.6 1.1 copy.15
  172.6 0.0 copy-start.1
  172.6 0.0 all-reduce.2.cloned.1.call-done
  172.6 0.1 copy-done.2
  172.7 2.2 %bitcast_dynamic-update-slice_fusion = (f32[1,72,4608]{2,1,0:T(8,128)}, f32[72,1152]{1,0:T(8,128)}, f32[72,1152]{1,0:T(8,128)}) fusion(f32[1,72,4608]{2,1,0:T(8,128)} %copy.15, s32[]{:T(128)S(6)} %select_n.2, f32[72,4608]{1,0:T(8,128)S(1)} %get-tuple-element.14, f32[72,1152]{1,0:T(8,128)S(1)} %copy-done.2, bf16[72,1152]{1,0:T(8,128)(2,1)} %all-reduce.2.cloned.1.call-done, ...), kind=kLoop, calls=%fused_computation.6 | loop fusion | flops 829440 | bytes 2156548 | tf_op jit(solution)/shard_map/dynamic_update_slice | solution.py:473
  174.9 0.0 copy-done.1
  174.9 1.2 copy.17
Async XLA Ops:
  7.2 165.5 %all-reduce.2.cloned.1.call-start = ((), (), s32[]{:S(2)}) async-start(), calls=%async_computation | async-start | bytes 331776 | tf_op jit(solution)/shard_map/psum | solution.py:463
  9.7 157.4 %copy-start = (f32[1,72,4608]{2,1,0:T(8,128)S(1)}, f32[1,72,4608]{2,1,0:T(8,128)}, u32[]{:S(2)}) copy-start(f32[1,72,4608]{2,1,0:T(8,128)} %param.10) | copy-start | bytes 3981316
  171.6 1.2 copy-start.2
  172.6 2.3 %copy-start.1 = (bf16[384,2304]{1,0:T(8,128)(2,1)S(1)}, bf16[384,2304]{1,0:T(8,128)(2,1)}, u32[]{:S(2)}) copy-start(bf16[384,2304]{1,0:T(8,128)(2,1)} %get-tuple-element.9) | copy-start | bytes 5308420
Sparse Core Ops, SparseCore 0:
  11.1 39.2 all-reduce.1

commit v3 on v2

--- a/solution.py
+++ b/solution.py
@@ -31,18 +31,19 @@
 
 
 def pair_kernel(
-    x_hbm, cot_hbm, p_ref,
-    out_ref, g_ref,
-    xb, cb, w, g, rah, raf, rbh, rbf, pws, pwr, gps, gpr, bks, bkr, tmp, acc,
+    frag_ref, x_hbm, cot_hbm, p_ref, snap_ref,
+    out_ref, g_ref, total_ref,
+    xb, cb, w, g, rah, raf, rbh, rbf, pws, pwr, gps, gpr, bks, bkr, tmp, acc, pair_tmp, ds, dr,
     loc_sem, ag_send, ag_recv, rs_send, rs_recv, pw_send, pw_recv,
-    x_send, x_recv, cot_send, cot_recv, bk_send, bk_recv, gp_send, gp_recv,
+    x_send, x_recv, cot_send, cot_recv, bk_send, bk_recv, gp_send, gp_recv, d_send, d_recv,
 ):
     tok, width = x_hbm.shape
     rows, ffw = p_ref.shape
     half_cols = ffw // 2
     n_chunks = half_cols // CHUNK
     block = 2 * rows
-    pad_rows = pwr.shape[2]
+    pad_rows = ds.shape[1]
+    frag = snap_ref.shape[1]
     cut = (block // 16 + 1) // 2 * 16
     n_x = x_send.shape[0]
     x_rows = tok // n_x
@@ -50,11 +51,12 @@
     bk_rows = tok // (n_bk // 2)
     bk_cols = width // 2
     scale = width ** (-0.5)
-    ahead = 4
+    ahead = 6
     work_lag = 10
     done = work_lag + n_chunks
 
     f = lax.axis_index("fsdp")
+    r = lax.axis_index("rep")
     yh = lax.rem(f, 2)
     x = lax.rem(lax.div(f, 2), 4)
     z = lax.div(f, 8)
@@ -63,6 +65,8 @@
         return {"fsdp": zz * 8 + xx * 2 + yy}
 
     peer = device(z, x, 1 - yh)
+    sibling = {"rep": r + 1 - 2 * lax.rem(r, 2)}
+    neighbour = {"rep": lax.rem(r + 2, 4)}
     place = {"x": x, "z": z}
     after = {a: lax.rem(place[a] + 1, 4) for a in place}
     before = {a: lax.rem(place[a] + 3, 4) for a in place}
@@ -145,8 +149,11 @@
     def bk_copy(i):
         return remote(bks.at[i], bkr.at[i], bk_send.at[i], bk_recv.at[i], peer)
 
-    def gp_copy(u):
-        return remote(gps.at[u], gpr.at[u], gp_send.at[u], gp_recv.at[u], peer)
+    def gp_copy(c):
+        return remote(gps.at[c], gpr.at[c], gp_send.at[c], gp_recv.at[c], peer)
+
+    def d_copy(i):
+        return remote(ds.at[i], dr.at[i], d_send.at[i], d_recv.at[i], (sibling, neighbour)[i])
 
     def own_x():
         return pltpu.make_async_copy(x_hbm, xb.at[pl.ds(0, tok)], loc_sem.at[n_chunks])
@@ -178,21 +185,28 @@
     each(n_chunks, lambda c: own_cot(c).start())
 
     def prepare(c):
+        parts = []
         for h in range(2):
             cols = pl.ds(pl.multiple_of(peer_base + c * CHUNK + h * LANES, LANES), LANES)
-            part = jnp.concatenate([p_ref[:, cols], jnp.zeros((pad_rows - rows, LANES), f32)], axis=0)
-            pws[c, h] = part.astype(bf16)
+            parts.append(p_ref[:, cols])
+        pws[c] = jnp.concatenate(parts, axis=0).astype(bf16)
 
     each(n_chunks, prepare)
+    local = p_ref[:, :frag]
+    for i in range(1, ffw // frag):
+        local = jnp.where(frag_ref[0] == i, p_ref[:, i * frag : (i + 1) * frag], local)
+    delta = snap_ref[...] - local
+    ds[0] = jnp.concatenate([delta, jnp.zeros((pad_rows - rows, frag), f32)], axis=0).astype(bf16)
 
     barrier = pltpu.get_barrier_semaphore()
-    partners = (peer, right["x"], left["x"], right["z"], left["z"])
+    partners = (peer, right["x"], left["x"], right["z"], left["z"], sibling, neighbour)
     for partner in partners:
         pl.semaphore_signal(barrier, inc=1, device_id=partner, device_id_type=MESH)
     pl.semaphore_wait(barrier, len(partners))
 
     each(n_chunks, lambda c: pw_copy(c).start())
     each(n_x, lambda i: x_copy(i).start())
+    d_copy(0).start()
 
     def chunk_weights(c):
         return jnp.concatenate(
@@ -207,10 +221,11 @@
 
     def gather_own(c):
         pw_copy(c).wait_recv()
+        pair_tmp[...] = pwr[c].astype(f32)
         for h in range(2):
             cols = pl.ds(pl.multiple_of(my_base + c * CHUNK + h * LANES, LANES), LANES)
             tmp[pl.ds(pl.multiple_of(yh * rows, 8), rows), :] = p_ref[:, cols]
-            tmp[pl.ds(pl.multiple_of((1 - yh) * rows, 8), rows), :] = pwr[c, h].astype(f32)[:rows]
+            tmp[pl.ds(pl.multiple_of((1 - yh) * rows, 8), rows), :] = pair_tmp[pl.ds(h * rows, rows), :]
             w[2 * c + h, z, x] = tmp[...].astype(bf16)
             gather_copy(2 * c + h, h, 0).start()
             gather_copy(2 * c + h, h, 1).start()
@@ -243,6 +258,21 @@
     def add_into(ref, other):
         ref[...] = (ref[...].astype(f32) + other[...].astype(f32)).astype(bf16)
 
+    def back_half(n, start):
+        part = jnp.concatenate(
+            [w[u, pl.ds(2 * n, 2)].reshape(bk_cols, LANES) for u in range(2 * n_chunks)], axis=1
+        )
+        return lax.dot_general(
+            cb[pl.ds(start, tok), :], part, (((1,), (1,)), ((), ())), preferred_element_type=f32
+        )
+
+    def send_back(n):
+        term = back_half(n, tok).astype(bf16)
+        for m in range(n_bk // 2):
+            i = n * (n_bk // 2) + m
+            bks[i] = term[m * bk_rows : (m + 1) * bk_rows]
+            bk_copy(i).start()
+
     def work(c):
         cot_copy(c).wait_recv()
 
@@ -251,6 +281,11 @@
             cot_copy(c + ahead).start()
 
         hidden(c, tok)
+
+        @pl.when(c == n_chunks - 1)
+        def _():
+            send_back(0)
+
         term = lax.dot_general(
             xb[...], cb[:, chunk_cols(c)], (((0,), (0,)), ((), ())), preferred_element_type=f32
         ).astype(bf16)
@@ -299,27 +334,13 @@
         scatter_copy(u, p, 7).wait_recv()
         mine = seg1(g, u, p, place[a])
         tmp[...] = mine[...].astype(f32) + rbf[u, 0].astype(f32) + rbf[u, 1].astype(f32)
-        theirs = tmp[pl.ds(pl.multiple_of((1 - yh) * rows, 8), rows), :]
-        theirs = jnp.concatenate([theirs, jnp.zeros((pad_rows - rows, LANES), f32)], axis=0)
-        gps[u] = theirs.astype(bf16)
-        gp_copy(u).start()
+        pair_tmp[pl.ds(p * rows, rows), :] = tmp[pl.ds(pl.multiple_of((1 - yh) * rows, 8), rows), :]
         cols = pl.ds(pl.multiple_of(my_base + u * LANES, LANES), LANES)
         g_ref[:, cols] = tmp[pl.ds(pl.multiple_of(yh * rows, 8), rows), :]
-
-    def back_half(n, start):
-        part = jnp.concatenate(
-            [w[u, pl.ds(2 * n, 2)].reshape(bk_cols, LANES) for u in range(2 * n_chunks)], axis=1
-        )
-        return lax.dot_general(
-            cb[pl.ds(start, tok), :], part, (((1,), (1,)), ((), ())), preferred_element_type=f32
-        )
-
-    def send_back(n):
-        term = back_half(n, tok).astype(bf16)
-        for m in range(n_bk // 2):
-            i = n * (n_bk // 2) + m
-            bks[i] = term[m * bk_rows : (m + 1) * bk_rows]
-            bk_copy(i).start()
+        if p == 1:
+            c = lax.div(u, 2)
+            gps[c] = pair_tmp[...].astype(bf16)
+            gp_copy(c).start()
 
     def keep_back(n):
         acc[n] = back_half(n, 0)
@@ -336,7 +357,16 @@
 
         ranged(t, 4, own_hidden)
 
-        @pl.when(t == 7)
+        @pl.when(t == 1)
+        def _():
+            d_copy(0).wait_recv()
+            ds[1] = (ds[0].astype(f32) + dr[0].astype(f32)).astype(bf16)
+
+        @pl.when(t == work_lag + 2)
+        def _():
+            d_copy(1).start()
+
+        @pl.when(t == 8)
         def _():
             for c in range(ahead):
                 cot_copy(c).start()
@@ -348,13 +378,13 @@
 
         ranged(t, work_lag, work)
 
-        @pl.when((t >= done) & (t < done + 2))
-        def _():
-            send_back(t - done)
-
-        @pl.when((t >= done + 2) & (t < done + 4))
-        def _():
-            keep_back(t - done - 2)
+        @pl.when(t == done)
+        def _():
+            send_back(1)
+
+        @pl.when((t >= done + 1) & (t < done + 3))
+        def _():
+            keep_back(t - done - 1)
 
         ranged(t, work_lag + 3, scatter_second)
         ranged(t, work_lag + 6, scatter_third)
@@ -372,19 +402,23 @@
 
     each(n_bk, finish_back)
 
-    def finish_grad(u):
-        gp_copy(u).wait_recv()
-        cols = pl.ds(pl.multiple_of(peer_base + u * LANES, LANES), LANES)
-        g_ref[:, cols] = gpr[u].astype(f32)[:rows]
-
-    each(2 * n_chunks, finish_grad)
+    def finish_grad(c):
+        gp_copy(c).wait_recv()
+        pair_tmp[...] = gpr[c].astype(f32)
+        for h in range(2):
+            cols = pl.ds(pl.multiple_of(peer_base + c * CHUNK + h * LANES, LANES), LANES)
+            g_ref[:, cols] = pair_tmp[pl.ds(h * rows, rows), :]
+
+    d_copy(1).wait_recv()
+    total_ref[...] = (ds[1].astype(f32) + dr[1].astype(f32))[:rows]
+    each(n_chunks, finish_grad)
 
     def settle(c):
         pw_copy(c).wait_send()
         cot_copy(c).wait_send()
+        gp_copy(c).wait_send()
         for p in range(2):
             u = 2 * c + p
-            gp_copy(u).wait_send()
             for k in range(8):
                 gather_copy(u, p, k).wait_send()
                 scatter_copy(u, p, k).wait_send()
@@ -392,11 +426,14 @@
     each(n_chunks, settle)
     each(n_x, lambda i: x_copy(i).wait_send())
     each(n_bk, lambda i: bk_copy(i).wait_send())
-
-
-def projection(acts, cot, weights):
+    for i in range(2):
+        d_copy(i).wait_send()
+
+
+def projection(fragment, acts, cot, weights, snapshot):
     tok, width = acts.shape
     rows, ffw = weights.shape
+    frag = snapshot.shape[1]
     units = ffw // 2 // LANES
     chunks = units // 2
     block = 2 * rows
@@ -409,13 +446,17 @@
         out_shape=(
             jax.ShapeDtypeStruct((tok, width), bf16),
             jax.ShapeDtypeStruct((rows, ffw), f32),
+            jax.ShapeDtypeStruct((rows, frag), f32),
         ),
         in_specs=[
+            pl.BlockSpec(memory_space=pltpu.SMEM),
             pl.BlockSpec(memory_space=pl.ANY),
             pl.BlockSpec(memory_space=pl.ANY),
             pl.BlockSpec(memory_space=pltpu.VMEM),
+            pl.BlockSpec(memory_space=pltpu.VMEM),
         ],
         out_specs=(
+            pl.BlockSpec(memory_space=pltpu.VMEM),
             pl.BlockSpec(memory_space=pltpu.VMEM),
             pl.BlockSpec(memory_space=pltpu.VMEM),
         ),
@@ -428,14 +469,17 @@
             vmem((units, 2, 4, block, LANES), bf16),
             vmem((units, block, LANES), bf16),
             vmem((units, 2, block, LANES), bf16),
-            vmem((chunks, 2, pad_rows, LANES), bf16),
-            vmem((chunks, 2, pad_rows, LANES), bf16),
-            vmem((units, pad_rows, LANES), bf16),
-            vmem((units, pad_rows, LANES), bf16),
+            vmem((chunks, block, LANES), bf16),
+            vmem((chunks, block, LANES), bf16),
+            vmem((chunks, block, LANES), bf16),
+            vmem((chunks, block, LANES), bf16),
             vmem((n_bk, tok // (n_bk // 2), width // 2), bf16),
             vmem((n_bk, tok // (n_bk // 2), width // 2), bf16),
             vmem((block, LANES), f32),
             vmem((2, tok, width // 2), f32),
+            vmem((block, LANES), f32),
+            vmem((2, pad_rows, frag), bf16),
+            vmem((2, pad_rows, frag), bf16),
             dma((chunks + 1,)),
             dma((units, 8)), dma((units, 8)),
             dma((units, 8)), dma((units, 8)),
@@ -443,7 +487,8 @@
             dma((n_x,)), dma((n_x,)),
             dma((chunks,)), dma((chunks,)),
             dma((n_bk,)), dma((n_bk,)),
-            dma((units,)), dma((units,)),
+            dma((chunks,)), dma((chunks,)),
+            dma((2,)), dma((2,)),
         ],
         compiler_params=pltpu.CompilerParams(
             collective_id=1, has_side_effects=True, vmem_limit_bytes=60 * 2**20
@@ -452,25 +497,59 @@
             flops=6 * tok * width * ffw, bytes_accessed=16 * tok * width, transcendentals=tok * ffw
         ),
         name="pair_projection",
-    )(acts, cot, weights)
+    )(fragment, acts, cot, weights, snapshot)
+
+
+def update_kernel(
+    frag_ref, g_ref, p_ref, m_ref, v_ref, snap_ref, mom_ref, total_ref,
+    new_p, new_m, new_v, new_mom, new_snap,
+):
+    step = pl.program_id(0)
+
+    @pl.when(step == 0)
+    def _():
+        outer = total_ref[...] * 0.25
+        mom = outer_mu * mom_ref[...] + outer
+        new_mom[...] = mom
+        new_snap[...] = snap_ref[...] - outer_rate * (outer + outer_mu * mom)
+
+    grad = g_ref[...]
+    weights = p_ref[...]
+    first = beta_one * m_ref[...] + (1.0 - beta_one) * grad
+    second = beta_two * v_ref[...] + (1.0 - beta_two) * grad * grad
+    new_m[...] = first
+    new_v[...] = second
+    stepped = weights - inner_rate * (first / (jnp.sqrt(second) + adam_eps) + decay_rate * weights)
+    new_p[...] = stepped
+
+    @pl.when(step == frag_ref[0])
+    def _():
+        new_p[...] = mix_rate * new_snap[...] + (1.0 - mix_rate) * new_p[...]
+
+
+def update(fragment, grad, weights, first, second, snapshot, momentum, total):
+    rows, ffw = weights.shape
+    frag = snapshot.shape[1]
+    wide = pl.BlockSpec((rows, frag), lambda j: (0, j))
+    fixed = pl.BlockSpec((rows, frag), lambda j: (0, 0))
+    full = jax.ShapeDtypeStruct((rows, ffw), f32)
+    part = jax.ShapeDtypeStruct((rows, frag), f32)
+    return pl.pallas_call(
+        update_kernel,
+        grid=(ffw // frag,),
+        in_specs=[pl.BlockSpec(memory_space=pltpu.SMEM)] + [wide] * 4 + [fixed] * 3,
+        out_specs=[wide] * 3 + [fixed] * 2,
+        out_shape=[full] * 3 + [part] * 2,
+        compiler_params=pltpu.CompilerParams(vmem_limit_bytes=60 * 2**20),
+        name="update",
+    )(fragment, grad, weights, first, second, snapshot, momentum, total)
 
 
 def body(inputs, cotangent, params, first_moment, second_moment, snapshot, momentum, fragment):
-    weights = params[0]
-    frag = snapshot.shape[1]
-    start_col = fragment[0] * frag
-    local = lax.dynamic_slice_in_dim(weights, start_col, frag, 1)
-    total = lax.psum((snapshot - local).astype(bf16), "rep").astype(f32)
-    input_grad, grad = projection(inputs[0], cotangent[0], weights)
-    outer_grad = total / lax.axis_size("rep")
-    new_momentum = outer_mu * momentum + outer_grad
-    new_snapshot = snapshot - outer_rate * (outer_grad + outer_mu * new_momentum)
-    first = beta_one * first_moment[0] + (1.0 - beta_one) * grad
-    second = beta_two * second_moment[0] + (1.0 - beta_two) * grad * grad
-    stepped = weights - inner_rate * (first / (jnp.sqrt(second) + adam_eps) + decay_rate * weights)
-    frag_part = lax.dynamic_slice_in_dim(stepped, start_col, frag, 1)
-    merged = mix_rate * new_snapshot + (1.0 - mix_rate) * frag_part
-    stepped = lax.dynamic_update_slice_in_dim(stepped, merged, start_col, 1)
+    input_grad, grad, total = projection(fragment, inputs[0], cotangent[0], params[0], snapshot)
+    stepped, first, second, new_momentum, new_snapshot = update(
+        fragment, grad, params[0], first_moment[0], second_moment[0], snapshot, momentum, total
+    )
     return (stepped[None], first[None], second[None], input_grad[None], new_momentum, new_snapshot)
 
 

time: 183 us -> 159 us (0.87)
  between operations: 14.7 us -> 0.66 us
  other arithmetic: 8.5 us -> 0 us
    pallas_call x1, Pallas kernels: 157 us -> 150 us  [projection(): pl.pallas_call(pair_kernel, out_shape=(jax.ShapeDtypeStruct((tok, width),...]
    pallas_call x0 -> x1, Pallas kernels: none -> 6.06 us  [update(): pl.pallas_call(update_kernel, grid=(ffw // frag,), in_specs=[pl.BlockSpec...]
    broadcast_in_dim x1 -> x0, other arithmetic: 4.53 us -> none  [body(): second[None]]
    dynamic_update_slice x1 -> x0, other arithmetic: 2.2 us -> none  [body(): stepped = lax.dynamic_update_slice_in_dim(stepped, merged, start_col, 1)]
  transfers between devices with their start and end apart: 1 -> 0, of which waited for: 0 -> 0; matrix products, arithmetic and copies ran while one was open for 3% -> 0% of each run, Pallas kernels for 86% -> 0%
where the time goes in v3:
time: 159 us; the launch traced here: 158 us
  Pallas kernels  156 us (98%)
    pallas_call x1, Pallas kernels, projection(): pl.pallas_call(pair_kernel, out_shape=(jax.ShapeDtypeStruct((tok, width),...  150 us
    pallas_call x1, Pallas kernels, update(): pl.pallas_call(update_kernel, grid=(ffw // frag,), in_specs=[pl.BlockSpec...  6.06 us

profile of v3, /device:TPU:0, one launch (start us, length us, event | category | flops | bytes accessed | tf_op | source)
XLA Modules:
  0.0 157.6 jit_solution(18249082695689990584)
XLA Ops:
  0.6 149.7 %pair_projection.1 = (bf16[384,2304]{1,0:T(8,128)(2,1)}, f32[72,4608]{1,0:T(8,128)}, f32[72,1152]{1,0:T(8,128)}) custom-call(s32[4]{0:T(128)} %frag_ref.3, bf16[384,2304]{1,0:T(8,128)(2,1)} %bitcast.15, bf16[384,4608]{1,0:T(8,128)(2,1)} %bitcast.14, f32[72,4608]{1,0:T(8,128)} %bitcast.10, f32[72,1152]{1,0:T(8,128)} %snap_ref.3), custom_call_target="tpu_custom_call" | custom-call | flops 24461180928 | bytes 14155776 | tf_op jit(solution)/shard_map/pair_projection/pallas_call | solution.py:444
  150.3 0.0 copy-start
  150.3 6.1 %update.1 = (f32[72,4608]{1,0:T(8,128)}, f32[72,4608]{1,0:T(8,128)}, f32[72,4608]{1,0:T(8,128)}, f32[72,1152]{1,0:T(8,128)}, f32[72,1152]{1,0:T(8,128)}) custom-call(s32[4]{0:T(128)} %frag_ref.3, f32[72,4608]{1,0:T(8,128)} %get-tuple-element.14.g_ref, f32[72,4608]{1,0:T(8,128)} %bitcast.11, f32[72,4608]{1,0:T(8,128)} %bitcast.12, f32[72,4608]{1,0:T(8,128)} %bitcast.13, ...), custom_call_target="tpu_custom_call" | custom-call | tf_op jit(solution)/shard_map/update/pallas_call | solution.py:537
  156.4 0.0 copy-done
  156.4 1.2 copy.15
Async XLA Ops:
  150.3 6.1 %copy-start = (bf16[384,2304]{1,0:T(8,128)(2,1)S(1)}, bf16[384,2304]{1,0:T(8,128)(2,1)}, u32[]{:S(2)}) copy-start(bf16[384,2304]{1,0:T(8,128)(2,1)} %get-tuple-element.19) | copy-start | bytes 5308420

commit v4 on v3

--- a/solution.py
+++ b/solution.py
@@ -31,11 +31,13 @@
 
 
 def pair_kernel(
-    frag_ref, x_hbm, cot_hbm, p_ref, snap_ref,
-    out_ref, g_ref, total_ref,
+    frag_ref, x_hbm, cot_hbm, p_hbm, snap_hbm,
+    out_hbm, g_hbm, total_hbm,
+    p_ref, snap_ref, out_ref, g_ref, total_ref,
     xb, cb, w, g, rah, raf, rbh, rbf, pws, pwr, gps, gpr, bks, bkr, tmp, acc, pair_tmp, ds, dr,
     loc_sem, ag_send, ag_recv, rs_send, rs_recv, pw_send, pw_recv,
     x_send, x_recv, cot_send, cot_recv, bk_send, bk_recv, gp_send, gp_recv, d_send, d_recv,
+    out_sem, g_sem, total_sem,
 ):
     tok, width = x_hbm.shape
     rows, ffw = p_ref.shape
@@ -152,11 +154,30 @@
     def gp_copy(c):
         return remote(gps.at[c], gpr.at[c], gp_send.at[c], gp_recv.at[c], peer)
 
+    def g_out(c, base, h):
+        cols = pl.ds(pl.multiple_of(base + c * CHUNK, CHUNK), CHUNK)
+        return pltpu.make_async_copy(g_ref.at[:, cols], g_hbm.at[:, cols], g_sem.at[2 * c + h])
+
+    def total_out():
+        return pltpu.make_async_copy(total_ref, total_hbm, total_sem.at[0])
+
+    def back_out(i):
+        n, m = lax.div(i, n_bk // 2), lax.rem(i, n_bk // 2)
+        at = pl.ds(pl.multiple_of(m * bk_rows, 16), bk_rows)
+        cols = pl.ds(pl.multiple_of(n * bk_cols, LANES), bk_cols)
+        return pltpu.make_async_copy(out_ref.at[at, cols], out_hbm.at[at, cols], out_sem.at[i])
+
     def d_copy(i):
         return remote(ds.at[i], dr.at[i], d_send.at[i], d_recv.at[i], (sibling, neighbour)[i])
 
     def own_x():
         return pltpu.make_async_copy(x_hbm, xb.at[pl.ds(0, tok)], loc_sem.at[n_chunks])
+
+    def own_params():
+        return pltpu.make_async_copy(p_hbm, p_ref, loc_sem.at[n_chunks + 1])
+
+    def own_snap():
+        return pltpu.make_async_copy(snap_hbm, snap_ref, loc_sem.at[n_chunks + 2])
 
     def own_cot(c):
         cols = pl.ds(pl.multiple_of(my_base + c * CHUNK, CHUNK), CHUNK)
@@ -181,8 +202,16 @@
                 step(2 * c + p, p)
         return run
 
+    barrier = pltpu.get_barrier_semaphore()
+    partners = (peer, right["x"], left["x"], right["z"], left["z"], sibling, neighbour)
+    for partner in partners:
+        pl.semaphore_signal(barrier, inc=1, device_id=partner, device_id_type=MESH)
+    own_params().start()
+    own_snap().start()
     own_x().start()
     each(n_chunks, lambda c: own_cot(c).start())
+    own_params().wait()
+    pl.semaphore_wait(barrier, len(partners))
 
     def prepare(c):
         parts = []
@@ -190,22 +219,17 @@
             cols = pl.ds(pl.multiple_of(peer_base + c * CHUNK + h * LANES, LANES), LANES)
             parts.append(p_ref[:, cols])
         pws[c] = jnp.concatenate(parts, axis=0).astype(bf16)
+        pw_copy(c).start()
 
     each(n_chunks, prepare)
+    each(n_x, lambda i: x_copy(i).start())
+    own_snap().wait()
     local = p_ref[:, :frag]
     for i in range(1, ffw // frag):
         local = jnp.where(frag_ref[0] == i, p_ref[:, i * frag : (i + 1) * frag], local)
     delta = snap_ref[...] - local
     ds[0] = jnp.concatenate([delta, jnp.zeros((pad_rows - rows, frag), f32)], axis=0).astype(bf16)
 
-    barrier = pltpu.get_barrier_semaphore()
-    partners = (peer, right["x"], left["x"], right["z"], left["z"], sibling, neighbour)
-    for partner in partners:
-        pl.semaphore_signal(barrier, inc=1, device_id=partner, device_id_type=MESH)
-    pl.semaphore_wait(barrier, len(partners))
-
-    each(n_chunks, lambda c: pw_copy(c).start())
-    each(n_x, lambda i: x_copy(i).start())
     d_copy(0).start()
 
     def chunk_weights(c):
@@ -258,22 +282,36 @@
     def add_into(ref, other):
         ref[...] = (ref[...].astype(f32) + other[...].astype(f32)).astype(bf16)
 
-    def back_half(n, start):
+    def back_part(n, start, units):
         part = jnp.concatenate(
-            [w[u, pl.ds(2 * n, 2)].reshape(bk_cols, LANES) for u in range(2 * n_chunks)], axis=1
+            [w[u, pl.ds(2 * n, 2)].reshape(bk_cols, LANES) for u in units], axis=1
         )
+        cols = slice(units[0] * LANES, (units[-1] + 1) * LANES)
         return lax.dot_general(
-            cb[pl.ds(start, tok), :], part, (((1,), (1,)), ((), ())), preferred_element_type=f32
+            cb[pl.ds(start, tok), cols], part, (((1,), (1,)), ((), ())), preferred_element_type=f32
         )
 
-    def send_back(n):
-        term = back_half(n, tok).astype(bf16)
+    def send_back(n, term):
         for m in range(n_bk // 2):
             i = n * (n_bk // 2) + m
-            bks[i] = term[m * bk_rows : (m + 1) * bk_rows]
+            bks[i] = term[m * bk_rows : (m + 1) * bk_rows].astype(bf16)
             bk_copy(i).start()
 
+    middle = n_chunks // 2
+    early = range(2 * middle)
+    late = range(2 * middle, 2 * n_chunks - 2)
+    final = range(2 * n_chunks - 2, 2 * n_chunks)
+
     def work(c):
+        @pl.when(c == middle)
+        def _():
+            acc[0] = back_part(0, tok, early)
+
+        @pl.when(c == n_chunks - 1)
+        def _():
+            d_copy(1).start()
+            acc[0] = acc[0] + back_part(0, tok, late)
+
         cot_copy(c).wait_recv()
 
         @pl.when(c + ahead < n_chunks)
@@ -284,7 +322,7 @@
 
         @pl.when(c == n_chunks - 1)
         def _():
-            send_back(0)
+            send_back(0, acc[0] + back_part(0, tok, final))
 
         term = lax.dot_general(
             xb[...], cb[:, chunk_cols(c)], (((0,), (0,)), ((), ())), preferred_element_type=f32
@@ -330,6 +368,8 @@
     @both
     def scatter_end(u, p):
         a = first_axis[p]
+        for k in range(6):
+            scatter_copy(u, p, k).wait_send()
         scatter_copy(u, p, 6).wait_recv()
         scatter_copy(u, p, 7).wait_recv()
         mine = seg1(g, u, p, place[a])
@@ -341,9 +381,17 @@
             c = lax.div(u, 2)
             gps[c] = pair_tmp[...].astype(bf16)
             gp_copy(c).start()
+            g_out(c, my_base, 0).start()
 
     def keep_back(n):
-        acc[n] = back_half(n, 0)
+        acc[n] = back_part(n, 0, range(2 * n_chunks))
+
+    def settle(c):
+        pw_copy(c).wait_send()
+        cot_copy(c).wait_send()
+        for p in range(2):
+            for k in range(8):
+                gather_copy(2 * c + p, p, k).wait_send()
 
     def tick(t):
         ranged(t, 0, gather_own)
@@ -362,10 +410,6 @@
             d_copy(0).wait_recv()
             ds[1] = (ds[0].astype(f32) + dr[0].astype(f32)).astype(bf16)
 
-        @pl.when(t == work_lag + 2)
-        def _():
-            d_copy(1).start()
-
         @pl.when(t == 8)
         def _():
             for c in range(ahead):
@@ -380,12 +424,13 @@
 
         @pl.when(t == done)
         def _():
-            send_back(1)
+            send_back(1, back_part(1, tok, range(2 * n_chunks)))
 
         @pl.when((t >= done + 1) & (t < done + 3))
         def _():
             keep_back(t - done - 1)
 
+        ranged(t, work_lag + 2, settle)
         ranged(t, work_lag + 3, scatter_second)
         ranged(t, work_lag + 6, scatter_third)
         ranged(t, work_lag + 8, scatter_fourth)
@@ -399,8 +444,11 @@
         at = pl.ds(pl.multiple_of(m * bk_rows, 16), bk_rows)
         cols = pl.ds(pl.multiple_of(n * bk_cols, LANES), bk_cols)
         out_ref[at, cols] = (acc[n, at, :] + bkr[i].astype(f32)).astype(bf16)
-
-    each(n_bk, finish_back)
+        back_out(i).start()
+
+    d_copy(1).wait_recv()
+    total_ref[...] = (ds[1].astype(f32) + dr[1].astype(f32))[:rows]
+    total_out().start()
 
     def finish_grad(c):
         gp_copy(c).wait_recv()
@@ -408,26 +456,30 @@
         for h in range(2):
             cols = pl.ds(pl.multiple_of(peer_base + c * CHUNK + h * LANES, LANES), LANES)
             g_ref[:, cols] = pair_tmp[pl.ds(h * rows, rows), :]
-
-    d_copy(1).wait_recv()
-    total_ref[...] = (ds[1].astype(f32) + dr[1].astype(f32))[:rows]
+        g_out(c, peer_base, 1).start()
+
+    each(n_bk, finish_back)
     each(n_chunks, finish_grad)
 
-    def settle(c):
-        pw_copy(c).wait_send()
-        cot_copy(c).wait_send()
+    def finish(c):
         gp_copy(c).wait_send()
         for p in range(2):
-            u = 2 * c + p
-            for k in range(8):
-                gather_copy(u, p, k).wait_send()
-                scatter_copy(u, p, k).wait_send()
-
-    each(n_chunks, settle)
+            for k in range(6, 8):
+                scatter_copy(2 * c + p, p, k).wait_send()
+        g_out(c, my_base, 0).wait()
+        g_out(c, peer_base, 1).wait()
+
+    each(n_chunks, finish)
     each(n_x, lambda i: x_copy(i).wait_send())
-    each(n_bk, lambda i: bk_copy(i).wait_send())
     for i in range(2):
         d_copy(i).wait_send()
+    total_out().wait()
+
+    def finish_out(i):
+        bk_copy(i).wait_send()
+        back_out(i).wait()
+
+    each(n_bk, finish_out)
 
 
 def projection(fragment, acts, cot, weights, snapshot):
@@ -452,15 +504,20 @@
             pl.BlockSpec(memory_space=pltpu.SMEM),
             pl.BlockSpec(memory_space=pl.ANY),
             pl.BlockSpec(memory_space=pl.ANY),
-            pl.BlockSpec(memory_space=pltpu.VMEM),
-            pl.BlockSpec(memory_space=pltpu.VMEM),
+            pl.BlockSpec(memory_space=pl.ANY),
+            pl.BlockSpec(memory_space=pl.ANY),
         ],
         out_specs=(
-            pl.BlockSpec(memory_space=pltpu.VMEM),
-            pl.BlockSpec(memory_space=pltpu.VMEM),
-            pl.BlockSpec(memory_space=pltpu.VMEM),
+            pl.BlockSpec(memory_space=pl.ANY),
+            pl.BlockSpec(memory_space=pl.ANY),
+            pl.BlockSpec(memory_space=pl.ANY),
         ),
         scratch_shapes=[
+            vmem((rows, ffw), f32),
+            vmem((rows, frag), f32),
+            vmem((tok, width), bf16),
+            vmem((rows, ffw), f32),
+            vmem((rows, frag), f32),
             vmem((2 * tok, width), bf16),
             vmem((2 * tok, ffw // 2), bf16),
             vmem((units, 4, 4, block, LANES), bf16),
@@ -480,7 +537,7 @@
             vmem((block, LANES), f32),
             vmem((2, pad_rows, frag), bf16),
             vmem((2, pad_rows, frag), bf16),
-            dma((chunks + 1,)),
+            dma((chunks + 3,)),
             dma((units, 8)), dma((units, 8)),
             dma((units, 8)), dma((units, 8)),
             dma((chunks,)), dma((chunks,)),
@@ -489,6 +546,7 @@
             dma((n_bk,)), dma((n_bk,)),
             dma((chunks,)), dma((chunks,)),
             dma((2,)), dma((2,)),
+            dma((n_bk,)), dma((units,)), dma((1,)),
         ],
         compiler_params=pltpu.CompilerParams(
             collective_id=1, has_side_effects=True, vmem_limit_bytes=60 * 2**20
@@ -501,54 +559,51 @@
 
 
 def update_kernel(
-    frag_ref, g_ref, p_ref, m_ref, v_ref, snap_ref, mom_ref, total_ref,
-    new_p, new_m, new_v, new_mom, new_snap,
+    frag_ref, g_ref, p_ref, m_ref, v_ref, snap_ref, mom_ref, total_ref, back_hbm,
+    new_p, new_m, new_v, new_mom, new_snap, out_hbm, sem,
 ):
-    step = pl.program_id(0)
-
-    @pl.when(step == 0)
-    def _():
-        outer = total_ref[...] * 0.25
-        mom = outer_mu * mom_ref[...] + outer
-        new_mom[...] = mom
-        new_snap[...] = snap_ref[...] - outer_rate * (outer + outer_mu * mom)
-
+    pass_on = pltpu.make_async_copy(back_hbm, out_hbm, sem)
+    pass_on.start()
+    frag = snap_ref.shape[1]
+    outer = total_ref[...] * 0.25
+    mom = outer_mu * mom_ref[...] + outer
+    new_mom[...] = mom
+    snap = snap_ref[...] - outer_rate * (outer + outer_mu * mom)
+    new_snap[...] = snap
     grad = g_ref[...]
     weights = p_ref[...]
     first = beta_one * m_ref[...] + (1.0 - beta_one) * grad
     second = beta_two * v_ref[...] + (1.0 - beta_two) * grad * grad
     new_m[...] = first
     new_v[...] = second
-    stepped = weights - inner_rate * (first / (jnp.sqrt(second) + adam_eps) + decay_rate * weights)
-    new_p[...] = stepped
-
-    @pl.when(step == frag_ref[0])
-    def _():
-        new_p[...] = mix_rate * new_snap[...] + (1.0 - mix_rate) * new_p[...]
-
-
-def update(fragment, grad, weights, first, second, snapshot, momentum, total):
-    rows, ffw = weights.shape
-    frag = snapshot.shape[1]
-    wide = pl.BlockSpec((rows, frag), lambda j: (0, j))
-    fixed = pl.BlockSpec((rows, frag), lambda j: (0, 0))
-    full = jax.ShapeDtypeStruct((rows, ffw), f32)
-    part = jax.ShapeDtypeStruct((rows, frag), f32)
+    new_p[...] = weights - inner_rate * (
+        first / (jnp.sqrt(second) + adam_eps) + decay_rate * weights
+    )
+    at = pl.ds(pl.multiple_of(frag_ref[0] * frag, LANES), frag)
+    new_p[:, at] = mix_rate * snap + (1.0 - mix_rate) * new_p[:, at]
+    pass_on.wait()
+
+
+def update(fragment, grad, weights, first, second, snapshot, momentum, total, back):
+    full = jax.ShapeDtypeStruct(weights.shape, f32)
+    part = jax.ShapeDtypeStruct(snapshot.shape, f32)
+    vmem = pl.BlockSpec(memory_space=pltpu.VMEM)
+    hbm = pl.BlockSpec(memory_space=pl.ANY)
     return pl.pallas_call(
         update_kernel,
-        grid=(ffw // frag,),
-        in_specs=[pl.BlockSpec(memory_space=pltpu.SMEM)] + [wide] * 4 + [fixed] * 3,
-        out_specs=[wide] * 3 + [fixed] * 2,
-        out_shape=[full] * 3 + [part] * 2,
+        in_specs=[pl.BlockSpec(memory_space=pltpu.SMEM)] + [vmem] * 7 + [hbm],
+        out_specs=[vmem] * 5 + [hbm],
+        out_shape=[full] * 3 + [part] * 2 + [jax.ShapeDtypeStruct(back.shape, back.dtype)],
+        scratch_shapes=[pltpu.SemaphoreType.DMA],
         compiler_params=pltpu.CompilerParams(vmem_limit_bytes=60 * 2**20),
         name="update",
-    )(fragment, grad, weights, first, second, snapshot, momentum, total)
+    )(fragment, grad, weights, first, second, snapshot, momentum, total, back)
 
 
 def body(inputs, cotangent, params, first_moment, second_moment, snapshot, momentum, fragment):
-    input_grad, grad, total = projection(fragment, inputs[0], cotangent[0], params[0], snapshot)
-    stepped, first, second, new_momentum, new_snapshot = update(
-        fragment, grad, params[0], first_moment[0], second_moment[0], snapshot, momentum, total
+    back, grad, total = projection(fragment, inputs[0], cotangent[0], params[0], snapshot)
+    stepped, first, second, new_momentum, new_snapshot, input_grad = update(
+        fragment, grad, params[0], first_moment[0], second_moment[0], snapshot, momentum, total, back
     )
     return (stepped[None], first[None], second[None], input_grad[None], new_momentum, new_snapshot)
 

time: 159 us -> 208 us (1.31)
  Pallas kernels: 156 us -> 207 us
    pallas_call x1, Pallas kernels: 6.06 us -> 59.6 us  [update(): pl.pallas_call(update_kernel, in_specs=[pl.BlockSpec(memory_space=pltpu.S...]
    pallas_call x1, Pallas kernels: 150 us -> 148 us  [projection(): pl.pallas_call(pair_kernel, out_shape=(jax.ShapeDtypeStruct((tok, width),...]
where the time goes in v4:
time: 208 us
  Pallas kernels  207 us (100%)
    pallas_call x1, Pallas kernels, projection(): pl.pallas_call(pair_kernel, out_shape=(jax.ShapeDtypeStruct((tok, width),...  148 us
    pallas_call x1, Pallas kernels, update(): pl.pallas_call(update_kernel, in_specs=[pl.BlockSpec(memory_space=pltpu.S...  59.6 us

profile of v4, /device:TPU:0, one launch (start us, length us, event | category | flops | bytes accessed | tf_op | source)
XLA Modules:
  0.0 207.9 jit_solution(9356878275412210004)
XLA Ops:
  0.6 147.5 %pair_projection.1 = (bf16[384,2304]{1,0:T(8,128)(2,1)}, f32[72,4608]{1,0:T(8,128)}, f32[72,1152]{1,0:T(8,128)}) custom-call(s32[4]{0:T(128)} %frag_ref.3, bf16[384,2304]{1,0:T(8,128)(2,1)} %bitcast.14, bf16[384,4608]{1,0:T(8,128)(2,1)} %bitcast.13, f32[72,4608]{1,0:T(8,128)} %bitcast.9, f32[72,1152]{1,0:T(8,128)} %snap_ref.1), custom_call_target="tpu_custom_call" | custom-call | flops 24461180928 | bytes 14155776 | tf_op jit(solution)/shard_map/pair_projection/pallas_call | solution.py:496
  148.1 59.6 %update.1 = (f32[72,4608]{1,0:T(8,128)}, f32[72,4608]{1,0:T(8,128)}, f32[72,4608]{1,0:T(8,128)}, f32[72,1152]{1,0:T(8,128)}, f32[72,1152]{1,0:T(8,128)}, /*index=5*/bf16[384,2304]{1,0:T(8,128)(2,1)}) custom-call(s32[4]{0:T(128)} %frag_ref.3, f32[72,4608]{1,0:T(8,128)} %get-tuple-element.15.g_ref, f32[72,4608]{1,0:T(8,128)} %bitcast.10, f32[72,4608]{1,0:T(8,128)} %bitcast.11, ...), custom_call_target="tpu_custom_call" | custom-call | tf_op jit(solution)/shard_map/update/pallas_call | solution.py:592

commit v5 on v4

--- a/solution.py
+++ b/solution.py
@@ -34,7 +34,7 @@
     frag_ref, x_hbm, cot_hbm, p_hbm, snap_hbm,
     out_hbm, g_hbm, total_hbm,
     p_ref, snap_ref, out_ref, g_ref, total_ref,
-    xb, cb, w, g, rah, raf, rbh, rbf, pws, pwr, gps, gpr, bks, bkr, tmp, acc, pair_tmp, ds, dr,
+    xb, cb, w, g, rah, raf, rbh, rbf, pws, pwr, gps, gpr, bks, bkr, tmp, acc, pair_tmp, ds, dr, dq, dt, du,
     loc_sem, ag_send, ag_recv, rs_send, rs_recv, pw_send, pw_recv,
     x_send, x_recv, cot_send, cot_recv, bk_send, bk_recv, gp_send, gp_recv, d_send, d_recv,
     out_sem, g_sem, total_sem,
@@ -45,6 +45,9 @@
     n_chunks = half_cols // CHUNK
     block = 2 * rows
     pad_rows = ds.shape[1]
+    part_rows = dq.shape[0]
+    core = lax.rem(lax.axis_index("rep"), 2)
+    part = pl.ds(pl.multiple_of(core * (pad_rows - part_rows), 16), part_rows)
     frag = snap_ref.shape[1]
     cut = (block // 16 + 1) // 2 * 16
     n_x = x_send.shape[0]
@@ -168,7 +171,12 @@
         return pltpu.make_async_copy(out_ref.at[at, cols], out_hbm.at[at, cols], out_sem.at[i])
 
     def d_copy(i):
-        return remote(ds.at[i], dr.at[i], d_send.at[i], d_recv.at[i], (sibling, neighbour)[i])
+        src, dst, to = (
+            (ds.at[0], dr, sibling),
+            (ds.at[1, part], dq, neighbour),
+            (dt, du, sibling),
+        )[i]
+        return remote(src, dst, d_send.at[i], d_recv.at[i], to)
 
     def own_x():
         return pltpu.make_async_copy(x_hbm, xb.at[pl.ds(0, tok)], loc_sem.at[n_chunks])
@@ -408,7 +416,7 @@
         @pl.when(t == 1)
         def _():
             d_copy(0).wait_recv()
-            ds[1] = (ds[0].astype(f32) + dr[0].astype(f32)).astype(bf16)
+            ds[1] = (ds[0].astype(f32) + dr[...].astype(f32)).astype(bf16)
 
         @pl.when(t == 8)
         def _():
@@ -446,9 +454,6 @@
         out_ref[at, cols] = (acc[n, at, :] + bkr[i].astype(f32)).astype(bf16)
         back_out(i).start()
 
-    d_copy(1).wait_recv()
-    total_ref[...] = (ds[1].astype(f32) + dr[1].astype(f32))[:rows]
-    total_out().start()
 
     def finish_grad(c):
         gp_copy(c).wait_recv()
@@ -458,7 +463,17 @@
             g_ref[:, cols] = pair_tmp[pl.ds(h * rows, rows), :]
         g_out(c, peer_base, 1).start()
 
+    d_copy(1).wait_recv()
+    dt[...] = ds[1, part].astype(f32) + dq[...].astype(f32)
+    d_copy(2).start()
     each(n_bk, finish_back)
+    d_copy(2).wait_recv()
+    total_ref[...] = jnp.where(
+        core == 0,
+        jnp.concatenate([dt[...], du[2 * part_rows - pad_rows :]], axis=0)[:rows],
+        jnp.concatenate([du[...], dt[2 * part_rows - pad_rows :]], axis=0)[:rows],
+    )
+    total_out().start()
     each(n_chunks, finish_grad)
 
     def finish(c):
@@ -471,7 +486,7 @@
 
     each(n_chunks, finish)
     each(n_x, lambda i: x_copy(i).wait_send())
-    for i in range(2):
+    for i in range(3):
         d_copy(i).wait_send()
     total_out().wait()
 
@@ -490,6 +505,7 @@
     chunks = units // 2
     block = 2 * rows
     pad_rows = (rows + 15) // 16 * 16
+    part_rows = (pad_rows // 16 + 1) // 2 * 16
     n_x, n_bk = 3, 6
     dma = pltpu.SemaphoreType.DMA
     vmem = pltpu.VMEM
@@ -536,7 +552,10 @@
             vmem((2, tok, width // 2), f32),
             vmem((block, LANES), f32),
             vmem((2, pad_rows, frag), bf16),
-            vmem((2, pad_rows, frag), bf16),
+            vmem((pad_rows, frag), bf16),
+            vmem((part_rows, frag), bf16),
+            vmem((part_rows, frag), f32),
+            vmem((part_rows, frag), f32),
             dma((chunks + 3,)),
             dma((units, 8)), dma((units, 8)),
             dma((units, 8)), dma((units, 8)),
@@ -545,7 +564,7 @@
             dma((chunks,)), dma((chunks,)),
             dma((n_bk,)), dma((n_bk,)),
             dma((chunks,)), dma((chunks,)),
-            dma((2,)), dma((2,)),
+            dma((3,)), dma((3,)),
             dma((n_bk,)), dma((units,)), dma((1,)),
         ],
         compiler_params=pltpu.CompilerParams(
@@ -560,16 +579,19 @@
 
 def update_kernel(
     frag_ref, g_ref, p_ref, m_ref, v_ref, snap_ref, mom_ref, total_ref, back_hbm,
-    new_p, new_m, new_v, new_mom, new_snap, out_hbm, sem,
+    new_p, new_m, new_v, new_mom, new_snap, out_hbm, held, sem,
 ):
-    pass_on = pltpu.make_async_copy(back_hbm, out_hbm, sem)
-    pass_on.start()
+    bring = pltpu.make_async_copy(back_hbm, held, sem.at[0])
+    pass_on = pltpu.make_async_copy(held, out_hbm, sem.at[1])
+    bring.start()
     frag = snap_ref.shape[1]
     outer = total_ref[...] * 0.25
     mom = outer_mu * mom_ref[...] + outer
     new_mom[...] = mom
     snap = snap_ref[...] - outer_rate * (outer + outer_mu * mom)
     new_snap[...] = snap
+    bring.wait()
+    pass_on.start()
     grad = g_ref[...]
     weights = p_ref[...]
     first = beta_one * m_ref[...] + (1.0 - beta_one) * grad
@@ -594,7 +616,7 @@
         in_specs=[pl.BlockSpec(memory_space=pltpu.SMEM)] + [vmem] * 7 + [hbm],
         out_specs=[vmem] * 5 + [hbm],
         out_shape=[full] * 3 + [part] * 2 + [jax.ShapeDtypeStruct(back.shape, back.dtype)],
-        scratch_shapes=[pltpu.SemaphoreType.DMA],
+        scratch_shapes=[pltpu.VMEM(back.shape, back.dtype), pltpu.SemaphoreType.DMA((2,))],
         compiler_params=pltpu.CompilerParams(vmem_limit_bytes=60 * 2**20),
         name="update",
     )(fragment, grad, weights, first, second, snapshot, momentum, total, back)

time: 208 us -> 155 us (0.75)
  Pallas kernels: 207 us -> 154 us
    pallas_call x1, Pallas kernels: 59.6 us -> 8.06 us  [update(): pl.pallas_call(update_kernel, in_specs=[pl.BlockSpec(memory_space=pltpu.S...]
where the time goes in v5:
time: 155 us
  Pallas kernels  154 us (99%)
    pallas_call x1, Pallas kernels, projection(): pl.pallas_call(pair_kernel, out_shape=(jax.ShapeDtypeStruct((tok, width),...  146 us
    pallas_call x1, Pallas kernels, update(): pl.pallas_call(update_kernel, in_specs=[pl.BlockSpec(memory_space=pltpu.S...  8.06 us

profile of v5, /device:TPU:0, one launch (start us, length us, event | category | flops | bytes accessed | tf_op | source)
XLA Modules:
  0.0 154.8 jit_solution(11937223014074007080)
XLA Ops:
  0.6 146.0 %pair_projection.1 = (bf16[384,2304]{1,0:T(8,128)(2,1)}, f32[72,4608]{1,0:T(8,128)}, f32[72,1152]{1,0:T(8,128)}) custom-call(s32[4]{0:T(128)} %frag_ref.3, bf16[384,2304]{1,0:T(8,128)(2,1)} %bitcast.14, bf16[384,4608]{1,0:T(8,128)(2,1)} %bitcast.13, f32[72,4608]{1,0:T(8,128)} %bitcast.9, f32[72,1152]{1,0:T(8,128)} %snap_ref.1), custom_call_target="tpu_custom_call" | custom-call | flops 24461180928 | bytes 14155776 | tf_op jit(solution)/shard_map/pair_projection/pallas_call | solution.py:512
  146.6 8.1 %update.1 = (f32[72,4608]{1,0:T(8,128)}, f32[72,4608]{1,0:T(8,128)}, f32[72,4608]{1,0:T(8,128)}, f32[72,1152]{1,0:T(8,128)}, f32[72,1152]{1,0:T(8,128)}, /*index=5*/bf16[384,2304]{1,0:T(8,128)(2,1)}) custom-call(s32[4]{0:T(128)} %frag_ref.3, f32[72,4608]{1,0:T(8,128)} %get-tuple-element.15.g_ref, f32[72,4608]{1,0:T(8,128)} %bitcast.10, f32[72,4608]{1,0:T(8,128)} %bitcast.11, ...), custom_call_target="tpu_custom_call" | custom-call | tf_op jit(solution)/shard_map/update/pallas_call | solution.py:614

commit v6 on v5

--- a/solution.py
+++ b/solution.py
@@ -32,12 +32,11 @@
 
 def pair_kernel(
     frag_ref, x_hbm, cot_hbm, p_hbm, snap_hbm,
-    out_hbm, g_hbm, total_hbm,
-    p_ref, snap_ref, out_ref, g_ref, total_ref,
+    out_ref, g_ref, total_ref,
+    p_ref, snap_ref,
     xb, cb, w, g, rah, raf, rbh, rbf, pws, pwr, gps, gpr, bks, bkr, tmp, acc, pair_tmp, ds, dr, dq, dt, du,
     loc_sem, ag_send, ag_recv, rs_send, rs_recv, pw_send, pw_recv,
     x_send, x_recv, cot_send, cot_recv, bk_send, bk_recv, gp_send, gp_recv, d_send, d_recv,
-    out_sem, g_sem, total_sem,
 ):
     tok, width = x_hbm.shape
     rows, ffw = p_ref.shape
@@ -157,19 +156,6 @@
     def gp_copy(c):
         return remote(gps.at[c], gpr.at[c], gp_send.at[c], gp_recv.at[c], peer)
 
-    def g_out(c, base, h):
-        cols = pl.ds(pl.multiple_of(base + c * CHUNK, CHUNK), CHUNK)
-        return pltpu.make_async_copy(g_ref.at[:, cols], g_hbm.at[:, cols], g_sem.at[2 * c + h])
-
-    def total_out():
-        return pltpu.make_async_copy(total_ref, total_hbm, total_sem.at[0])
-
-    def back_out(i):
-        n, m = lax.div(i, n_bk // 2), lax.rem(i, n_bk // 2)
-        at = pl.ds(pl.multiple_of(m * bk_rows, 16), bk_rows)
-        cols = pl.ds(pl.multiple_of(n * bk_cols, LANES), bk_cols)
-        return pltpu.make_async_copy(out_ref.at[at, cols], out_hbm.at[at, cols], out_sem.at[i])
-
     def d_copy(i):
         src, dst, to = (
             (ds.at[0], dr, sibling),
@@ -181,11 +167,12 @@
     def own_x():
         return pltpu.make_async_copy(x_hbm, xb.at[pl.ds(0, tok)], loc_sem.at[n_chunks])
 
-    def own_params():
-        return pltpu.make_async_copy(p_hbm, p_ref, loc_sem.at[n_chunks + 1])
+    def own_params(h):
+        cols = pl.ds(pl.multiple_of((my_base, peer_base)[h], LANES), half_cols)
+        return pltpu.make_async_copy(p_hbm.at[:, cols], p_ref.at[:, cols], loc_sem.at[n_chunks + 2 + h])
 
     def own_snap():
-        return pltpu.make_async_copy(snap_hbm, snap_ref, loc_sem.at[n_chunks + 2])
+        return pltpu.make_async_copy(snap_hbm, snap_ref, loc_sem.at[n_chunks + 1])
 
     def own_cot(c):
         cols = pl.ds(pl.multiple_of(my_base + c * CHUNK, CHUNK), CHUNK)
@@ -214,11 +201,10 @@
     partners = (peer, right["x"], left["x"], right["z"], left["z"], sibling, neighbour)
     for partner in partners:
         pl.semaphore_signal(barrier, inc=1, device_id=partner, device_id_type=MESH)
-    own_params().start()
+    own_params(1).start()
+    own_params(0).start()
     own_snap().start()
-    own_x().start()
-    each(n_chunks, lambda c: own_cot(c).start())
-    own_params().wait()
+    own_params(1).wait()
     pl.semaphore_wait(barrier, len(partners))
 
     def prepare(c):
@@ -231,7 +217,10 @@
 
     each(n_chunks, prepare)
     each(n_x, lambda i: x_copy(i).start())
+    own_x().start()
+    each(n_chunks, lambda c: own_cot(c).start())
     own_snap().wait()
+    own_params(0).wait()
     local = p_ref[:, :frag]
     for i in range(1, ffw // frag):
         local = jnp.where(frag_ref[0] == i, p_ref[:, i * frag : (i + 1) * frag], local)
@@ -389,7 +378,6 @@
             c = lax.div(u, 2)
             gps[c] = pair_tmp[...].astype(bf16)
             gp_copy(c).start()
-            g_out(c, my_base, 0).start()
 
     def keep_back(n):
         acc[n] = back_part(n, 0, range(2 * n_chunks))
@@ -452,7 +440,6 @@
         at = pl.ds(pl.multiple_of(m * bk_rows, 16), bk_rows)
         cols = pl.ds(pl.multiple_of(n * bk_cols, LANES), bk_cols)
         out_ref[at, cols] = (acc[n, at, :] + bkr[i].astype(f32)).astype(bf16)
-        back_out(i).start()
 
 
     def finish_grad(c):
@@ -461,7 +448,6 @@
         for h in range(2):
             cols = pl.ds(pl.multiple_of(peer_base + c * CHUNK + h * LANES, LANES), LANES)
             g_ref[:, cols] = pair_tmp[pl.ds(h * rows, rows), :]
-        g_out(c, peer_base, 1).start()
 
     d_copy(1).wait_recv()
     dt[...] = ds[1, part].astype(f32) + dq[...].astype(f32)
@@ -473,7 +459,6 @@
         jnp.concatenate([dt[...], du[2 * part_rows - pad_rows :]], axis=0)[:rows],
         jnp.concatenate([du[...], dt[2 * part_rows - pad_rows :]], axis=0)[:rows],
     )
-    total_out().start()
     each(n_chunks, finish_grad)
 
     def finish(c):
@@ -481,18 +466,14 @@
         for p in range(2):
             for k in range(6, 8):
                 scatter_copy(2 * c + p, p, k).wait_send()
-        g_out(c, my_base, 0).wait()
-        g_out(c, peer_base, 1).wait()
 
     each(n_chunks, finish)
     each(n_x, lambda i: x_copy(i).wait_send())
     for i in range(3):
         d_copy(i).wait_send()
-    total_out().wait()
 
     def finish_out(i):
         bk_copy(i).wait_send()
-        back_out(i).wait()
 
     each(n_bk, finish_out)
 
@@ -512,9 +493,9 @@
     return pl.pallas_call(
         pair_kernel,
         out_shape=(
-            jax.ShapeDtypeStruct((tok, width), bf16),
-            jax.ShapeDtypeStruct((rows, ffw), f32),
-            jax.ShapeDtypeStruct((rows, frag), f32),
+            vmem((tok, width), bf16),
+            vmem((rows, ffw), f32),
+            vmem((rows, frag), f32),
         ),
         in_specs=[
             pl.BlockSpec(memory_space=pltpu.SMEM),
@@ -523,15 +504,8 @@
             pl.BlockSpec(memory_space=pl.ANY),
             pl.BlockSpec(memory_space=pl.ANY),
         ],
-        out_specs=(
-            pl.BlockSpec(memory_space=pl.ANY),
-            pl.BlockSpec(memory_space=pl.ANY),
-            pl.BlockSpec(memory_space=pl.ANY),
-        ),
+        out_specs=(pl.BlockSpec(memory_space=vmem),) * 3,
         scratch_shapes=[
-            vmem((rows, ffw), f32),
-            vmem((rows, frag), f32),
-            vmem((tok, width), bf16),
             vmem((rows, ffw), f32),
             vmem((rows, frag), f32),
             vmem((2 * tok, width), bf16),
@@ -556,7 +530,7 @@
             vmem((part_rows, frag), bf16),
             vmem((part_rows, frag), f32),
             vmem((part_rows, frag), f32),
-            dma((chunks + 3,)),
+            dma((chunks + 4,)),
             dma((units, 8)), dma((units, 8)),
             dma((units, 8)), dma((units, 8)),
             dma((chunks,)), dma((chunks,)),
@@ -565,10 +539,9 @@
             dma((n_bk,)), dma((n_bk,)),
             dma((chunks,)), dma((chunks,)),
             dma((3,)), dma((3,)),
-            dma((n_bk,)), dma((units,)), dma((1,)),
         ],
         compiler_params=pltpu.CompilerParams(
-            collective_id=1, has_side_effects=True, vmem_limit_bytes=60 * 2**20
+            collective_id=1, has_side_effects=True, vmem_limit_bytes=53 * 2**20
         ),
         cost_estimate=pl.CostEstimate(
             flops=6 * tok * width * ffw, bytes_accessed=16 * tok * width, transcendentals=tok * ffw
@@ -578,32 +551,45 @@
 
 
 def update_kernel(
-    frag_ref, g_ref, p_ref, m_ref, v_ref, snap_ref, mom_ref, total_ref, back_hbm,
-    new_p, new_m, new_v, new_mom, new_snap, out_hbm, held, sem,
+    frag_ref, g_ref, p_ref, m_ref, v_ref, snap_ref, mom_ref, total_ref, back_ref,
+    p_out, m_out, v_out, mom_out, snap_out, back_out,
+    new_p, new_m, new_v, new_mom, new_snap, wide_sem, sem,
 ):
-    bring = pltpu.make_async_copy(back_hbm, held, sem.at[0])
-    pass_on = pltpu.make_async_copy(held, out_hbm, sem.at[1])
-    bring.start()
     frag = snap_ref.shape[1]
+    blocks = wide_sem.shape[0]
+    step = p_ref.shape[0] // blocks
+    pass_on = pltpu.make_async_copy(back_ref, back_out, sem.at[0])
+    pass_on.start()
     outer = total_ref[...] * 0.25
     mom = outer_mu * mom_ref[...] + outer
     new_mom[...] = mom
-    snap = snap_ref[...] - outer_rate * (outer + outer_mu * mom)
-    new_snap[...] = snap
-    bring.wait()
-    pass_on.start()
-    grad = g_ref[...]
-    weights = p_ref[...]
-    first = beta_one * m_ref[...] + (1.0 - beta_one) * grad
-    second = beta_two * v_ref[...] + (1.0 - beta_two) * grad * grad
-    new_m[...] = first
-    new_v[...] = second
-    new_p[...] = weights - inner_rate * (
-        first / (jnp.sqrt(second) + adam_eps) + decay_rate * weights
-    )
-    at = pl.ds(pl.multiple_of(frag_ref[0] * frag, LANES), frag)
-    new_p[:, at] = mix_rate * snap + (1.0 - mix_rate) * new_p[:, at]
-    pass_on.wait()
+    new_snap[...] = snap_ref[...] - outer_rate * (outer + outer_mu * mom)
+    copies = [
+        pass_on,
+        pltpu.make_async_copy(new_mom, mom_out, sem.at[1]),
+        pltpu.make_async_copy(new_snap, snap_out, sem.at[2]),
+    ]
+    copies[1].start()
+    copies[2].start()
+    cols = pl.ds(pl.multiple_of(frag_ref[0] * frag, LANES), frag)
+    for b in range(blocks):
+        at = pl.ds(b * step, step)
+        grad = g_ref[at, :]
+        weights = p_ref[at, :]
+        first = beta_one * m_ref[at, :] + (1.0 - beta_one) * grad
+        second = beta_two * v_ref[at, :] + (1.0 - beta_two) * grad * grad
+        new_m[at, :] = first
+        new_v[at, :] = second
+        new_p[at, :] = weights - inner_rate * (
+            first / (jnp.sqrt(second) + adam_eps) + decay_rate * weights
+        )
+        new_p[at, cols] = mix_rate * new_snap[at, :] + (1.0 - mix_rate) * new_p[at, cols]
+        for i, (src, dst) in enumerate(((new_p, p_out), (new_m, m_out), (new_v, v_out))):
+            copy = pltpu.make_async_copy(src.at[at], dst.at[at], wide_sem.at[b, i])
+            copy.start()
+            copies.append(copy)
+    for copy in copies:
+        copy.wait()
 
 
 def update(fragment, grad, weights, first, second, snapshot, momentum, total, back):
@@ -613,11 +599,13 @@
     hbm = pl.BlockSpec(memory_space=pl.ANY)
     return pl.pallas_call(
         update_kernel,
-        in_specs=[pl.BlockSpec(memory_space=pltpu.SMEM)] + [vmem] * 7 + [hbm],
-        out_specs=[vmem] * 5 + [hbm],
+        in_specs=[pl.BlockSpec(memory_space=pltpu.SMEM)] + [vmem] * 8,
+        out_specs=[hbm] * 6,
         out_shape=[full] * 3 + [part] * 2 + [jax.ShapeDtypeStruct(back.shape, back.dtype)],
-        scratch_shapes=[pltpu.VMEM(back.shape, back.dtype), pltpu.SemaphoreType.DMA((2,))],
-        compiler_params=pltpu.CompilerParams(vmem_limit_bytes=60 * 2**20),
+        scratch_shapes=[pltpu.VMEM(weights.shape, f32)] * 3
+        + [pltpu.VMEM(snapshot.shape, f32)] * 2
+        + [pltpu.SemaphoreType.DMA((3, 3)), pltpu.SemaphoreType.DMA((3,))],
+        compiler_params=pltpu.CompilerParams(vmem_limit_bytes=24 * 2**20),
         name="update",
     )(fragment, grad, weights, first, second, snapshot, momentum, total, back)
 

time: 155 us -> 150 us (0.968)
  Pallas kernels: 154 us -> 149 us
    pallas_call x1, Pallas kernels: 8.06 us -> 3.51 us  [update(): pl.pallas_call(update_kernel, in_specs=[pl.BlockSpec(memory_space=pltpu.S...]
where the time goes in v6:
time: 150 us
  Pallas kernels  149 us (99%)
    pallas_call x1, Pallas kernels, projection(): pl.pallas_call(pair_kernel, out_shape=(vmem((tok, width), bf16), vmem((ro...  145 us
    pallas_call x1, Pallas kernels, update(): pl.pallas_call(update_kernel, in_specs=[pl.BlockSpec(memory_space=pltpu.S...  3.51 us

profile of v6, /device:TPU:0, one launch (start us, length us, event | category | flops | bytes accessed | tf_op | source)
XLA Modules:
  0.0 149.8 jit_solution(6988016401207379911)
XLA Ops:
  0.6 0.0 copy-start
  0.6 0.0 copy-start.1
  0.7 0.0 copy-start.2
  0.7 0.0 copy-start.3
  0.7 0.0 copy-start.4
  0.7 0.0 copy-start.5
  0.7 145.3 %pair_projection.1 = (bf16[384,2304]{1,0:T(8,128)(2,1)S(1)}, f32[72,4608]{1,0:T(8,128)S(1)}, f32[72,1152]{1,0:T(8,128)S(1)}) custom-call(s32[4]{0:T(128)} %frag_ref.3, bf16[384,2304]{1,0:T(8,128)(2,1)} %bitcast.14, bf16[384,4608]{1,0:T(8,128)(2,1)} %bitcast.13, f32[72,4608]{1,0:T(8,128)} %bitcast.9, f32[72,1152]{1,0:T(8,128)} %snap_ref.1), custom_call_target="tpu_custom_call" | custom-call | flops 24461180928 | bytes 14155776 | tf_op jit(solution)/shard_map/pair_projection/pallas_call | solution.py:493
  146.0 0.0 copy-done
  146.0 0.0 copy-done.1
  146.0 0.0 copy-done.2
  146.1 0.0 copy-done.3
  146.1 0.0 copy-done.4
  146.1 0.0 copy-done.5
  146.1 3.5 %update.1 = (f32[72,4608]{1,0:T(8,128)}, f32[72,4608]{1,0:T(8,128)}, f32[72,4608]{1,0:T(8,128)}, f32[72,1152]{1,0:T(8,128)}, f32[72,1152]{1,0:T(8,128)}, /*index=5*/bf16[384,2304]{1,0:T(8,128)(2,1)}) custom-call(s32[4]{0:T(128)S(1)} %copy-done.5, f32[72,4608]{1,0:T(8,128)S(1)} %get-tuple-element.15.g_ref, f32[72,4608]{1,0:T(8,128)S(1)} %bitcast.10, ...), custom_call_target="tpu_custom_call" | custom-call | tf_op jit(solution)/shard_map/update/pallas_call | solution.py:600
Async XLA Ops:
  0.6 145.4 %copy-start = (f32[1,72,4608]{2,1,0:T(8,128)S(1)}, f32[1,72,4608]{2,1,0:T(8,128)}, u32[]{:S(2)}) copy-start(f32[1,72,4608]{2,1,0:T(8,128)} %param.10) | copy-start | bytes 3981316
  0.6 145.4 %copy-start.1 = (f32[1,72,4608]{2,1,0:T(8,128)S(1)}, f32[1,72,4608]{2,1,0:T(8,128)}, u32[]{:S(2)}) copy-start(f32[1,72,4608]{2,1,0:T(8,128)} %param.11) | copy-start | bytes 3981316
  0.7 145.4 %copy-start.2 = (f32[1,72,4608]{2,1,0:T(8,128)S(1)}, f32[1,72,4608]{2,1,0:T(8,128)}, u32[]{:S(2)}) copy-start(f32[1,72,4608]{2,1,0:T(8,128)} %param.12) | copy-start | bytes 3981316
  0.7 145.4 %copy-start.3 = (f32[72,1152]{1,0:T(8,128)S(1)}, f32[72,1152]{1,0:T(8,128)}, u32[]{:S(2)}) copy-start(f32[72,1152]{1,0:T(8,128)} %snap_ref.1) | copy-start | bytes 995332
  0.7 145.4 %copy-start.4 = (f32[72,1152]{1,0:T(8,128)S(1)}, f32[72,1152]{1,0:T(8,128)}, u32[]{:S(2)}) copy-start(f32[72,1152]{1,0:T(8,128)} %mom_ref.1) | copy-start | bytes 995332
  0.7 145.4 %copy-start.5 = (s32[4]{0:T(128)S(1)}, s32[4]{0:T(128)}, u32[]{:S(2)}) copy-start(s32[4]{0:T(128)} %frag_ref.3) | copy-start | bytes 52

commit v7 on v6

--- a/solution.py
+++ b/solution.py
@@ -46,7 +46,7 @@
     pad_rows = ds.shape[1]
     part_rows = dq.shape[0]
     core = lax.rem(lax.axis_index("rep"), 2)
-    part = pl.ds(pl.multiple_of(core * (pad_rows - part_rows), 16), part_rows)
+    parts = (pl.ds(0, part_rows), pl.ds(part_rows, pad_rows - part_rows))
     frag = snap_ref.shape[1]
     cut = (block // 16 + 1) // 2 * 16
     n_x = x_send.shape[0]
@@ -159,10 +159,21 @@
     def d_copy(i):
         src, dst, to = (
             (ds.at[0], dr, sibling),
-            (ds.at[1, part], dq, neighbour),
             (dt, du, sibling),
         )[i]
         return remote(src, dst, d_send.at[i], d_recv.at[i], to)
+
+    def on_core(step):
+        for which, part in enumerate(parts):
+            count = part.size
+            copy = remote(
+                ds.at[1, part], dq.at[pl.ds(0, count)], d_send.at[2], d_recv.at[2], neighbour
+            )
+            pl.when(core == which)(functools.partial(step, copy, part, count))
+
+    def add_half(copy, part, count):
+        copy.wait_recv()
+        dt[:count] = ds[1, part].astype(f32) + dq[:count].astype(f32)
 
     def own_x():
         return pltpu.make_async_copy(x_hbm, xb.at[pl.ds(0, tok)], loc_sem.at[n_chunks])
@@ -306,7 +317,7 @@
 
         @pl.when(c == n_chunks - 1)
         def _():
-            d_copy(1).start()
+            on_core(lambda copy, part, count: copy.start())
             acc[0] = acc[0] + back_part(0, tok, late)
 
         cot_copy(c).wait_recv()
@@ -449,15 +460,14 @@
             cols = pl.ds(pl.multiple_of(peer_base + c * CHUNK + h * LANES, LANES), LANES)
             g_ref[:, cols] = pair_tmp[pl.ds(h * rows, rows), :]
 
+    on_core(add_half)
+    d_copy(1).start()
+    each(n_bk, finish_back)
     d_copy(1).wait_recv()
-    dt[...] = ds[1, part].astype(f32) + dq[...].astype(f32)
-    d_copy(2).start()
-    each(n_bk, finish_back)
-    d_copy(2).wait_recv()
     total_ref[...] = jnp.where(
         core == 0,
-        jnp.concatenate([dt[...], du[2 * part_rows - pad_rows :]], axis=0)[:rows],
-        jnp.concatenate([du[...], dt[2 * part_rows - pad_rows :]], axis=0)[:rows],
+        jnp.concatenate([dt[...], du[: pad_rows - part_rows]], axis=0)[:rows],
+        jnp.concatenate([du[...], dt[: pad_rows - part_rows]], axis=0)[:rows],
     )
     each(n_chunks, finish_grad)
 
@@ -469,8 +479,9 @@
 
     each(n_chunks, finish)
     each(n_x, lambda i: x_copy(i).wait_send())
-    for i in range(3):
+    for i in range(2):
         d_copy(i).wait_send()
+    on_core(lambda copy, part, count: copy.wait_send())
 
     def finish_out(i):
         bk_copy(i).wait_send()

time: 150 us -> 149 us (level)
  no operation moved by 1% of the time
where the time goes in v7:
time: 149 us
  Pallas kernels  148 us (99%)
    pallas_call x1, Pallas kernels, projection(): pl.pallas_call(pair_kernel, out_shape=(vmem((tok, width), bf16), vmem((ro...  145 us
    pallas_call x1, Pallas kernels, update(): pl.pallas_call(update_kernel, in_specs=[pl.BlockSpec(memory_space=pltpu.S...  3.51 us

profile of v7, /device:TPU:0, one launch (start us, length us, event | category | flops | bytes accessed | tf_op | source)
XLA Modules:
  0.0 149.2 jit_solution(13222372020269347426)
XLA Ops:
  0.6 0.0 copy-start
  0.6 0.0 copy-start.1
  0.7 0.0 copy-start.2
  0.7 0.0 copy-start.3
  0.7 0.0 copy-start.4
  0.7 0.0 copy-start.5
  0.7 144.7 %pair_projection.1 = (bf16[384,2304]{1,0:T(8,128)(2,1)S(1)}, f32[72,4608]{1,0:T(8,128)S(1)}, f32[72,1152]{1,0:T(8,128)S(1)}) custom-call(s32[4]{0:T(128)} %frag_ref.3, bf16[384,2304]{1,0:T(8,128)(2,1)} %bitcast.14, bf16[384,4608]{1,0:T(8,128)(2,1)} %bitcast.13, f32[72,4608]{1,0:T(8,128)} %bitcast.9, f32[72,1152]{1,0:T(8,128)} %snap_ref.1), custom_call_target="tpu_custom_call" | custom-call | flops 24461180928 | bytes 14155776 | tf_op jit(solution)/shard_map/pair_projection/pallas_call | solution.py:504
  145.4 0.0 copy-done
  145.5 0.0 copy-done.1
  145.5 0.0 copy-done.2
  145.5 0.0 copy-done.3
  145.5 0.0 copy-done.4
  145.5 0.0 copy-done.5
  145.5 3.5 %update.1 = (f32[72,4608]{1,0:T(8,128)}, f32[72,4608]{1,0:T(8,128)}, f32[72,4608]{1,0:T(8,128)}, f32[72,1152]{1,0:T(8,128)}, f32[72,1152]{1,0:T(8,128)}, /*index=5*/bf16[384,2304]{1,0:T(8,128)(2,1)}) custom-call(s32[4]{0:T(128)S(1)} %copy-done.5, f32[72,4608]{1,0:T(8,128)S(1)} %get-tuple-element.15.g_ref, f32[72,4608]{1,0:T(8,128)S(1)} %bitcast.10, ...), custom_call_target="tpu_custom_call" | custom-call | tf_op jit(solution)/shard_map/update/pallas_call | solution.py:611
Async XLA Ops:
  0.6 144.8 %copy-start = (f32[1,72,4608]{2,1,0:T(8,128)S(1)}, f32[1,72,4608]{2,1,0:T(8,128)}, u32[]{:S(2)}) copy-start(f32[1,72,4608]{2,1,0:T(8,128)} %param.10) | copy-start | bytes 3981316
  0.6 144.8 %copy-start.1 = (f32[1,72,4608]{2,1,0:T(8,128)S(1)}, f32[1,72,4608]{2,1,0:T(8,128)}, u32[]{:S(2)}) copy-start(f32[1,72,4608]{2,1,0:T(8,128)} %param.11) | copy-start | bytes 3981316
  0.7 144.8 %copy-start.2 = (f32[1,72,4608]{2,1,0:T(8,128)S(1)}, f32[1,72,4608]{2,1,0:T(8,128)}, u32[]{:S(2)}) copy-start(f32[1,72,4608]{2,1,0:T(8,128)} %param.12) | copy-start | bytes 3981316
  0.7 144.8 %copy-start.3 = (f32[72,1152]{1,0:T(8,128)S(1)}, f32[72,1152]{1,0:T(8,128)}, u32[]{:S(2)}) copy-start(f32[72,1152]{1,0:T(8,128)} %snap_ref.1) | copy-start | bytes 995332
  0.7 144.8 %copy-start.4 = (f32[72,1152]{1,0:T(8,128)S(1)}, f32[72,1152]{1,0:T(8,128)}, u32[]{:S(2)}) copy-start(f32[72,1152]{1,0:T(8,128)} %mom_ref.1) | copy-start | bytes 995332
  0.7 144.8 %copy-start.5 = (s32[4]{0:T(128)S(1)}, s32[4]{0:T(128)}, u32[]{:S(2)}) copy-start(s32[4]{0:T(128)} %frag_ref.3) | copy-start | bytes 52

commit v8 on v6

--- a/solution.py
+++ b/solution.py
@@ -44,9 +44,7 @@
     n_chunks = half_cols // CHUNK
     block = 2 * rows
     pad_rows = ds.shape[1]
-    part_rows = dq.shape[0]
     core = lax.rem(lax.axis_index("rep"), 2)
-    part = pl.ds(pl.multiple_of(core * (pad_rows - part_rows), 16), part_rows)
     frag = snap_ref.shape[1]
     cut = (block // 16 + 1) // 2 * 16
     n_x = x_send.shape[0]
@@ -159,10 +157,20 @@
     def d_copy(i):
         src, dst, to = (
             (ds.at[0], dr, sibling),
-            (ds.at[1, part], dq, neighbour),
             (dt, du, sibling),
         )[i]
         return remote(src, dst, d_send.at[i], d_recv.at[i], to)
+
+    def on_second(step):
+        pl.when(core == 1)(step)
+
+    def across_y():
+        return remote(ds.at[1], dq, d_send.at[2], d_recv.at[2], neighbour)
+
+    def add_chips():
+        across_y().wait_recv()
+        dt[...] = ds[1].astype(f32) + dq[...].astype(f32)
+        d_copy(1).start()
 
     def own_x():
         return pltpu.make_async_copy(x_hbm, xb.at[pl.ds(0, tok)], loc_sem.at[n_chunks])
@@ -306,7 +314,7 @@
 
         @pl.when(c == n_chunks - 1)
         def _():
-            d_copy(1).start()
+            on_second(lambda: across_y().start())
             acc[0] = acc[0] + back_part(0, tok, late)
 
         cot_copy(c).wait_recv()
@@ -449,16 +457,18 @@
             cols = pl.ds(pl.multiple_of(peer_base + c * CHUNK + h * LANES, LANES), LANES)
             g_ref[:, cols] = pair_tmp[pl.ds(h * rows, rows), :]
 
-    d_copy(1).wait_recv()
-    dt[...] = ds[1, part].astype(f32) + dq[...].astype(f32)
-    d_copy(2).start()
+    on_second(add_chips)
     each(n_bk, finish_back)
-    d_copy(2).wait_recv()
-    total_ref[...] = jnp.where(
-        core == 0,
-        jnp.concatenate([dt[...], du[2 * part_rows - pad_rows :]], axis=0)[:rows],
-        jnp.concatenate([du[...], dt[2 * part_rows - pad_rows :]], axis=0)[:rows],
-    )
+
+    @pl.when(core == 0)
+    def _():
+        d_copy(1).wait_recv()
+        total_ref[...] = du[...][:rows]
+
+    @pl.when(core == 1)
+    def _():
+        total_ref[...] = dt[...][:rows]
+
     each(n_chunks, finish_grad)
 
     def finish(c):
@@ -469,8 +479,9 @@
 
     each(n_chunks, finish)
     each(n_x, lambda i: x_copy(i).wait_send())
-    for i in range(3):
-        d_copy(i).wait_send()
+    d_copy(0).wait_send()
+    on_second(lambda: d_copy(1).wait_send())
+    on_second(lambda: across_y().wait_send())
 
     def finish_out(i):
         bk_copy(i).wait_send()
@@ -486,7 +497,6 @@
     chunks = units // 2
     block = 2 * rows
     pad_rows = (rows + 15) // 16 * 16
-    part_rows = (pad_rows // 16 + 1) // 2 * 16
     n_x, n_bk = 3, 6
     dma = pltpu.SemaphoreType.DMA
     vmem = pltpu.VMEM
@@ -527,9 +537,9 @@
             vmem((block, LANES), f32),
             vmem((2, pad_rows, frag), bf16),
             vmem((pad_rows, frag), bf16),
-            vmem((part_rows, frag), bf16),
-            vmem((part_rows, frag), f32),
-            vmem((part_rows, frag), f32),
+            vmem((pad_rows, frag), bf16),
+            vmem((pad_rows, frag), f32),
+            vmem((pad_rows, frag), f32),
             dma((chunks + 4,)),
             dma((units, 8)), dma((units, 8)),
             dma((units, 8)), dma((units, 8)),

time: 150 us -> 149 us (level)
  no operation moved by 1% of the time
where the time goes in v8:
time: 149 us
  Pallas kernels  148 us (99%)
    pallas_call x1, Pallas kernels, projection(): pl.pallas_call(pair_kernel, out_shape=(vmem((tok, width), bf16), vmem((ro...  145 us
    pallas_call x1, Pallas kernels, update(): pl.pallas_call(update_kernel, in_specs=[pl.BlockSpec(memory_space=pltpu.S...  3.51 us

profile of v8, /device:TPU:0, one launch (start us, length us, event | category | flops | bytes accessed | tf_op | source)
XLA Modules:
  0.0 149.2 jit_solution(15283682339348987478)
XLA Ops:
  0.6 0.0 copy-start
  0.6 0.0 copy-start.1
  0.7 0.0 copy-start.2
  0.7 0.0 copy-start.3
  0.7 0.0 copy-start.4
  0.7 0.0 copy-start.5
  0.7 144.7 %pair_projection.1 = (bf16[384,2304]{1,0:T(8,128)(2,1)S(1)}, f32[72,4608]{1,0:T(8,128)S(1)}, f32[72,1152]{1,0:T(8,128)S(1)}) custom-call(s32[4]{0:T(128)} %frag_ref.3, bf16[384,2304]{1,0:T(8,128)(2,1)} %bitcast.14, bf16[384,4608]{1,0:T(8,128)(2,1)} %bitcast.13, f32[72,4608]{1,0:T(8,128)} %bitcast.9, f32[72,1152]{1,0:T(8,128)} %snap_ref.1), custom_call_target="tpu_custom_call" | custom-call | flops 24461180928 | bytes 14155776 | tf_op jit(solution)/shard_map/pair_projection/pallas_call | solution.py:503
  145.4 0.0 copy-done
  145.5 0.0 copy-done.1
  145.5 0.0 copy-done.2
  145.5 0.0 copy-done.3
  145.5 0.0 copy-done.4
  145.5 0.0 copy-done.5
  145.5 3.5 %update.1 = (f32[72,4608]{1,0:T(8,128)}, f32[72,4608]{1,0:T(8,128)}, f32[72,4608]{1,0:T(8,128)}, f32[72,1152]{1,0:T(8,128)}, f32[72,1152]{1,0:T(8,128)}, /*index=5*/bf16[384,2304]{1,0:T(8,128)(2,1)}) custom-call(s32[4]{0:T(128)S(1)} %copy-done.5, f32[72,4608]{1,0:T(8,128)S(1)} %get-tuple-element.15.g_ref, f32[72,4608]{1,0:T(8,128)S(1)} %bitcast.10, ...), custom_call_target="tpu_custom_call" | custom-call | tf_op jit(solution)/shard_map/update/pallas_call | solution.py:610
Async XLA Ops:
  0.6 144.8 %copy-start = (f32[1,72,4608]{2,1,0:T(8,128)S(1)}, f32[1,72,4608]{2,1,0:T(8,128)}, u32[]{:S(2)}) copy-start(f32[1,72,4608]{2,1,0:T(8,128)} %param.10) | copy-start | bytes 3981316
  0.6 144.8 %copy-start.1 = (f32[1,72,4608]{2,1,0:T(8,128)S(1)}, f32[1,72,4608]{2,1,0:T(8,128)}, u32[]{:S(2)}) copy-start(f32[1,72,4608]{2,1,0:T(8,128)} %param.11) | copy-start | bytes 3981316
  0.7 144.8 %copy-start.2 = (f32[1,72,4608]{2,1,0:T(8,128)S(1)}, f32[1,72,4608]{2,1,0:T(8,128)}, u32[]{:S(2)}) copy-start(f32[1,72,4608]{2,1,0:T(8,128)} %param.12) | copy-start | bytes 3981316
  0.7 144.8 %copy-start.3 = (f32[72,1152]{1,0:T(8,128)S(1)}, f32[72,1152]{1,0:T(8,128)}, u32[]{:S(2)}) copy-start(f32[72,1152]{1,0:T(8,128)} %snap_ref.1) | copy-start | bytes 995332
  0.7 144.8 %copy-start.4 = (f32[72,1152]{1,0:T(8,128)S(1)}, f32[72,1152]{1,0:T(8,128)}, u32[]{:S(2)}) copy-start(f32[72,1152]{1,0:T(8,128)} %mom_ref.1) | copy-start | bytes 995332
  0.7 144.8 %copy-start.5 = (s32[4]{0:T(128)S(1)}, s32[4]{0:T(128)}, u32[]{:S(2)}) copy-start(s32[4]{0:T(128)} %frag_ref.3) | copy-start | bytes 52
